TPU v7x, 512 devices: a whole 4x8x8 slice. The times are simulated.
512 devices in a mesh: tm: 32 (over z_hi, x, core), space: 16 (over y, z_lo).
Axes of the slice: x: 4, y: 8, z: 8 (z_hi: 4, z_lo: 2; z = z_hi * 2 + z_lo), core: 2. Of those that a mesh axis runs over, the one named last changes fastest.
Arguments:
- incoming_features: bfloat16 [32, 256, 2048], P('tm', 'space'), may hold values from -6 to 6
- frame_noise_grades: int32 [32], replicated, may hold values from 0 to 999
- noise_affine_lookup: bfloat16 [1000, 4, 2048], P(None, None, ('tm', 'space')), may hold values from -3 to 3
- plane_projection_matrix: bfloat16 [2048, 3, 16, 128], P(None, None, 'space'), may hold values from -0.125 to 0.125
- plane_mixing_matrix: bfloat16 [16, 128, 2048], P('space'), may hold values from -0.125 to 0.125
- clock_projection_matrix: bfloat16 [2048, 3, 16, 128], P(None, None, 'space'), may hold values from -0.125 to 0.125
- logit_stretch_factors: float32 [2, 16], replicated, may hold values from 2 to 32, as said below
Outputs:
- mixed: bfloat16 [32, 256, 2048], P('tm', 'space')
- time_heads: bfloat16 [32, 256, 2048], P('tm', None, 'space')
Inputs may be any that keep to these rules, and one draw needn't show every extreme that they name: `logit_stretch_factors`: positive score scales of the heads.
All inputs are finite; a program needn't handle non-finite values.
Results may differ from a plain program's by a relative error of at most 0.04.
Values may be sent and summed in bfloat16 or wider, within the bound.
No kernel may reach another device: no remote copies, remote signals or barrier semaphores. Data moves between devices by JAX's collectives and lax.ppermute only.
A program may use at most 64 MiB of HBM per device.

v0:
```python
import math

import jax
import jax.numpy as jnp
from jax import lax
from jax.sharding import PartitionSpec as P


def layer_norm(token_rows):
    centre = token_rows - jnp.mean(token_rows, axis=-1, keepdims=True)
    spread = jnp.mean(centre * centre, axis=-1, keepdims=True)
    return centre * lax.rsqrt(spread + 1e-05)


def unit_rows(vectors):
    return vectors * lax.rsqrt(jnp.mean(vectors * vectors, axis=-1, keepdims=True) + 1e-06)


def soft_weights(scores):
    top_score = jnp.max(scores, axis=-1, keepdims=True)
    expo = jnp.exp(scores - top_score)
    return (expo / jnp.sum(expo, axis=-1, keepdims=True)).astype(jnp.bfloat16)


def qkv_rows(token_rows, scale_row, shift_row, weight):
    normed = (layer_norm(token_rows.astype(jnp.float32)) * (1.0 + scale_row) + shift_row).astype(
        jnp.bfloat16
    )
    flat = weight.reshape(weight.shape[0], -1)
    projected = jnp.dot(normed, flat, preferred_element_type=jnp.float32)
    projected = projected.reshape((token_rows.shape[0],) + weight.shape[1:])
    queries = unit_rows(projected[:, 0]).astype(jnp.bfloat16)
    keys = unit_rows(projected[:, 1]).astype(jnp.bfloat16)
    values = projected[:, 2].astype(jnp.bfloat16)
    return jnp.stack([queries, keys, values], axis=1)


def attend_space(packed, scales):
    queries = packed[:, 0]
    keys = packed[:, 1]
    values = packed[:, 2]
    length = packed.shape[0]
    q_span = math.gcd(length, 512)
    blocks = queries.reshape(length // q_span, q_span, queries.shape[1], queries.shape[2])

    def one_block(q_block):
        scores = (
            jnp.einsum("ihd,jhd->hij", q_block, keys, preferred_element_type=jnp.float32)
            * scales[:, None, None]
        )
        weights = soft_weights(scores)
        return jnp.einsum(
            "hij,jhd->ihd", weights, values, preferred_element_type=jnp.float32
        ).astype(jnp.bfloat16)

    return lax.map(one_block, blocks).reshape(length, -1)


def attend_time(packed, scales):
    queries = packed[:, :, 0]
    keys = packed[:, :, 1]
    values = packed[:, :, 2]
    scores = (
        jnp.einsum("fphd,gphd->phfg", queries, keys, preferred_element_type=jnp.float32)
        * scales[None, :, None, None]
    )
    frame_count = scores.shape[-1]
    causal = lax.broadcasted_iota(jnp.int32, (frame_count, frame_count), 0) >= lax.broadcasted_iota(
        jnp.int32, (frame_count, frame_count), 1
    )
    scores = jnp.where(causal[None, None], scores, -1e30)
    weights = soft_weights(scores)
    output = jnp.einsum(
        "phfg,gphd->fphd", weights, values, preferred_element_type=jnp.float32
    ).astype(jnp.bfloat16)
    return output.reshape(output.shape[0], output.shape[1], -1)


def body(
    incoming_features,
    frame_noise_grades,
    noise_affine_lookup,
    plane_projection_matrix,
    plane_mixing_matrix,
    clock_projection_matrix,
    logit_stretch_factors,
):
    width = incoming_features.shape[2]
    local_attn_groups = plane_projection_matrix.shape[2]
    attn_group_size = plane_projection_matrix.shape[3]
    local_cols = jnp.take(noise_affine_lookup, frame_noise_grades, axis=0)
    all_levels = lax.all_gather(local_cols, ("tm", "space"), axis=2, tiled=True)
    own_mod = lax.dynamic_slice_in_dim(all_levels, lax.axis_index("tm"), 1, 0)
    modulate = own_mod[0].astype(jnp.float32)
    first_attn_group = lax.axis_index("space") * local_attn_groups
    plane_stretch_factors = lax.dynamic_slice_in_dim(
        logit_stretch_factors[0] / attn_group_size, first_attn_group, local_attn_groups, 0
    )
    clock_stretch_factors = lax.dynamic_slice_in_dim(
        logit_stretch_factors[1] / attn_group_size, first_attn_group, local_attn_groups, 0
    )
    out_weight = plane_mixing_matrix.reshape(local_attn_groups * attn_group_size, width)
    frame_rows = incoming_features[0]
    packed = qkv_rows(
        lax.all_gather(incoming_features, "space", axis=1, tiled=True)[0],
        modulate[0],
        modulate[1],
        plane_projection_matrix,
    )[None][0]
    attended = attend_space(packed, plane_stretch_factors)
    branch_sum = lax.psum_scatter(
        jnp.dot(attended, out_weight, preferred_element_type=jnp.float32).astype(jnp.bfloat16),
        "space",
        scatter_dimension=0,
        tiled=True,
    ).astype(jnp.float32)
    mixed = (frame_rows.astype(jnp.float32) + branch_sum).astype(jnp.bfloat16)
    packed_time = qkv_rows(
        lax.all_gather(mixed, "space", axis=0, tiled=True),
        modulate[2],
        modulate[3],
        clock_projection_matrix,
    )
    all_frames = lax.all_to_all(packed_time[None], "tm", split_axis=1, concat_axis=0, tiled=True)
    moved = attend_time(all_frames, clock_stretch_factors)
    time_heads = lax.all_to_all(moved, "tm", split_axis=0, concat_axis=1, tiled=True)
    return (mixed[None], time_heads)


def solution(mesh):
    return jax.shard_map(
        body,
        mesh=mesh,
        in_specs=(
            P("tm", "space", None),
            P(),
            P(None, None, ("tm", "space")),
            P(None, None, "space", None),
            P("space", None, None),
            P(None, None, "space", None),
            P(),
        ),
        out_specs=(P("tm", "space", None), P("tm", None, "space")),
        check_vma=False,
    )
```

profile of v0, /device:TPU:1, one launch (start us, length us, event | category | flops | bytes accessed | tf_op | source)
XLA Modules:
  0.0 1490.9 jit_solution(11259249684317089921)
XLA Ops:
  7.2 0.0 copy-start
  7.2 0.0 all-gather.3.cloned.1.call-start
  7.2 0.7 all-gather.3.cloned.1.call-update
  7.9 0.0 reduce-scatter.2.cloned.1.call-start
  8.0 0.7 compare_select_fusion
  8.6 0.7 compare_and_fusion
  9.3 0.0 copy-start.5
  9.3 2.0 copy.22
  11.3 0.6 gather_fusion
  11.9 0.1 broadcast_select_fusion
  12.0 0.1 copy.23
  12.1 1.7 copy.24
  13.9 0.0 copy-done.5
  13.9 0.6 constant_dynamic-slice_fusion.1
  14.5 1231.4 %all_gather.10 = bf16[32,4,2048]{0,1,2:T(4,128)(2,1)S(1)} all-gather(bf16[32,4,4]{0,1,2:T(4,128)(2,1)S(1)} %copy.23), channel_id=1, replica_groups=mesh['tm'=32,'space'=16] {'tm','space'}, dimensions={2}, use_global_device_ids=true | all-gather | bytes 525312 | tf_op jit(solution)/shard_map/all_gather | solution.py:92
  1245.9 1.2 dynamic-slice_convert_fusion
  1247.1 17.9 %fusion.42 = (f32[2048]{0:T(1024)S(1)}, f32[2048]{0:T(1024)S(1)}, f32[2048]{0:T(1024)S(1)}, f32[2048]{0:T(1024)S(1)}) fusion(f32[1,4,2048]{0,1,2:T(4,128)S(1)} %dynamic-slice_convert_fusion), kind=kLoop, calls=%fused_computation.52 | loop fusion | flops 4096 | bytes 65536 | tf_op jit(solution)/shard_map/add | solution.py:26
  1265.0 0.0 all-gather.3.cloned.1.call-done
  1265.1 0.0 copy-start.1
  1265.1 1.5 convert_reduce_fusion
  1266.6 1.6 fusion.13
  1268.3 0.0 copy-done.1
  1268.3 0.8 fusion.18
  1269.1 0.0 copy-start.4
  1269.1 0.0 copy-start.3
  1269.2 1.0 fusion.62
  1270.2 0.1 fusion.44
  1270.2 1.6 convolution_convert_fusion
  1271.9 0.0 reduce-scatter.2.cloned.1.call-update
  1271.9 0.2 all-gather.5.cloned.1.call-start
  1272.2 82.3 %reduce-scatter.2.cloned.1.call-done = bf16[16,2048]{1,0:T(8,128)(2,1)} async-done(((bf16[256,2048]{1,0:T(8,128)(2,1)}), bf16[16,2048]{1,0:T(8,128)(2,1)}) %reduce-scatter.2.cloned.1.call-update) | async-done | bytes 65552 | tf_op jit(solution)/shard_map/reduce_scatter | solution.py:111
  1354.4 0.0 copy-done.4
  1354.4 1.5 fusion.45
  1355.9 0.0 all-gather.5.cloned.1.call-update
  1355.9 1.6 copy.25
  1357.5 71.0 %all-gather.5.cloned.1.call-done = bf16[256,2048]{1,0:T(8,128)(2,1)} async-done(((bf16[16,2048]{1,0:T(8,128)(2,1)}), bf16[256,2048]{1,0:T(8,128)(2,1)}) %all-gather.5.cloned.1.call-update) | async-done | bytes 1048592 | tf_op jit(solution)/shard_map/all_gather | solution.py:119
  1428.6 1.5 convert_reduce_fusion.1
  1430.1 1.6 fusion.3
  1431.8 2.2 fusion.21
  1434.1 0.9 copy.26
  1435.0 20.3 %all-to-all-start = ((bf16[1,256,3,1,128]{4,2,3,0,1:T(4,128)(2,1)}), bf16[1,256,3,1,128]{4,2,3,0,1:T(4,128)(2,1)S(1)}, u32[]{:S(2)}, u32[]{:S(2)}) async-start(bf16[1,256,3,1,128]{4,2,3,0,1:T(4,128)(2,1)} %copy.26), calls=%async_computation.1 | async-start | bytes 524288 | tf_op jit(solution)/shard_map/all_to_all | solution.py:124
  1455.3 0.6 constant_dynamic-slice_fusion
  1455.9 12.5 all-to-all-done
  1468.4 0.8 fusion.26
  1469.2 0.1 fusion.63
  1469.2 0.2 fusion.28
  1469.5 14.2 all_to_all.24
  1483.7 0.6 copy.46
  (22 shorter events, 0.3 us)
Async XLA Ops:
  7.2 1263.1 %copy-start = (bf16[1,128,2048]{2,1,0:T(8,128)(2,1)S(1)}, bf16[1,128,2048]{2,1,0:T(8,128)(2,1)}, u32[]{:S(2)}) copy-start(bf16[1,128,2048]{2,1,0:T(8,128)(2,1)} %param.11) | copy-start | bytes 1572868
  7.2 1257.9 %all-gather.3.cloned.1.call-start = ((), (), s32[]{:S(2)}) async-start(), calls=%async_computation.3 | async-start | bytes 1114112 | tf_op jit(solution)/shard_map/all_gather | solution.py:105
  7.9 1346.5 %reduce-scatter.2.cloned.1.call-start = ((), (), s32[]{:S(2)}) async-start(), calls=%async_computation.4 | async-start | bytes 1114112 | tf_op jit(solution)/shard_map/reduce_scatter | solution.py:111
  9.3 4.6 copy-start.5
  1265.1 3.2 copy-start.1
  1269.1 85.4 %copy-start.4 = (bf16[1,16,2048]{2,1,0:T(8,128)(2,1)S(1)}, bf16[1,16,2048]{2,1,0:T(8,128)(2,1)}, u32[]{:S(2)}) copy-start(bf16[1,16,2048]{2,1,0:T(8,128)(2,1)} %param.7) | copy-start | bytes 196612
  1269.1 86.8 %copy-start.3 = (bf16[2048,3,1,128]{3,0,2,1:T(8,128)(2,1)S(1)}, bf16[2048,3,1,128]{3,0,2,1:T(8,128)(2,1)}, u32[]{:S(2)}) copy-start(bf16[2048,3,1,128]{3,0,2,1:T(8,128)(2,1)} %param.12) | copy-start | bytes 4718596
  1271.9 156.6 %all-gather.5.cloned.1.call-start = ((), (), s32[]{:S(2)}) async-start(), calls=%async_computation.5 | async-start | bytes 1114112 | tf_op jit(solution)/shard_map/all_gather | solution.py:119
  1428.6 3.2 copy-start.2
  1435.0 33.4 %all-to-all-start = ((bf16[1,256,3,1,128]{4,2,3,0,1:T(4,128)(2,1)}), bf16[1,256,3,1,128]{4,2,3,0,1:T(4,128)(2,1)S(1)}, u32[]{:S(2)}, u32[]{:S(2)}) async-start(bf16[1,256,3,1,128]{4,2,3,0,1:T(4,128)(2,1)} %copy.26), calls=%async_computation.1 | async-start | bytes 524288 | tf_op jit(solution)/shard_map/all_to_all | solution.py:124
Sparse Core Ops, SparseCore 0:
  10.1 67.7 all-gather.2
  1272.0 82.3 reduce-scatter.1
  1357.3 71.2 all-gather.4
where the time goes:
time: 1490 us
  blocking collectives  1250 us (84%)
  waiting for transfers between devices  166 us (11%)
  other arithmetic  28.7 us (2%)
  starting transfers between devices  20.6 us (1%)
    all_gather x1, blocking collectives, body(): all_levels = lax.all_gather(local_cols, ('tm', 'space'), axis=2, tiled=True)  1230 us
    reduce_scatter x1, waiting for transfers between devices, body(): lax.psum_scatter(jnp.dot(attended, out_weight, preferred_element_type=jnp...  82.3 us
    all_gather x1, waiting for transfers between devices, body(): lax.all_gather(mixed, 'space', axis=0, tiled=True)  71 us
  transfers between devices with their start and end apart: 4, of which 3 were waited for; matrix products, arithmetic and copies ran while one was open for 2% of the time, Pallas kernels for 0%

commit v1 on v0

v1 whole, which is shorter than its diff:
```python
import functools

import jax
import jax.numpy as jnp
from jax import lax
from jax.experimental import pallas as pl
from jax.experimental.pallas import tpu as pltpu
from jax.sharding import Mesh
from jax.sharding import PartitionSpec as P

TM = ("zh", "x", "core")
VMEM_LIMIT = 48 * 1024 * 1024
BF16 = jnp.bfloat16
F32 = jnp.float32


def iota(shape, dim):
    return lax.broadcasted_iota(jnp.int32, shape, dim)


def dot(a, b, dims=((1,), (0,))):
    return lax.dot_general(a, b, (dims, ((), ())), preferred_element_type=F32)


def call(kernel, out, *args, in_smem=(), flops=0, scratch=()):
    specs = [
        pl.BlockSpec(memory_space=pltpu.SMEM if i in in_smem else pltpu.VMEM) for i in range(len(args))
    ]
    outs = jax.tree.map(lambda _: pl.BlockSpec(memory_space=pltpu.VMEM), out)
    total = sum(a.size * a.dtype.itemsize for a in args)
    return pl.pallas_call(
        kernel,
        out_shape=out,
        in_specs=specs,
        out_specs=outs,
        scratch_shapes=scratch,
        compiler_params=pltpu.CompilerParams(vmem_limit_bytes=VMEM_LIMIT),
        cost_estimate=pl.CostEstimate(flops=flops, bytes_accessed=total, transcendentals=0),
    )(*args)


def pack_kernel(grades_ref, table_ref, x_ref, out_ref):
    levels, frames = table_ref.shape[2], grades_ref.shape[1]
    hot = jnp.where(iota((levels, frames), 0) == grades_ref[...], 1.0, 0.0).astype(BF16)
    base = lax.rem(lax.axis_index("y"), 4) * 16
    placed = jnp.zeros((frames, 128), F32)
    for k in range(4):
        picked = dot(table_ref[k], hot).astype(BF16)
        lane = iota((4, 128), 0) + (base + 4 * k)
        place = jnp.where((iota((4, 128), 1) & 63) == lane, 1.0, 0.0).astype(BF16)
        placed = placed + dot(picked, place, ((0,), (0,)))
    packed = jnp.where(iota((16, 128), 1) < 64, placed[0:16], placed[16:32]).astype(BF16)
    for j in range(8):
        out_ref[j, :, 0:2048] = x_ref[0]
        out_ref[j, :, 2048:2176] = packed


def frame_rows_kernel(gathered_ref, out_ref):
    low, high = (
        sum(gathered_ref[4 * half + i, :, 2048:2176].astype(F32) for i in range(4)) for half in range(2)
    )
    left = iota((16, 128), 1) < 64
    first = jnp.where(left, low, pltpu.roll(high, 64, 1))
    second = jnp.where(left, pltpu.roll(low, 64, 1), high)
    rows = jnp.concatenate([first, second, first, second], axis=0)
    out_ref[...] = rows.astype(BF16)


def modulation(rows_ref):
    values = jnp.concatenate([rows_ref[0:32, :], rows_ref[32:64, :]], axis=1)
    n = iota((256, 256), 1)
    source = ((n >> 2) & 1) * 128 + ((n >> 3) & 7) * 16 + (n >> 6) * 4 + (n & 3)
    permute = jnp.where(iota((256, 256), 0) == source, 1.0, 0.0).astype(BF16)
    ordered = dot(values, permute).astype(BF16)
    own_block = (iota((32, 2048), 1) >> 6) == iota((32, 2048), 0)
    rows = []
    for k in range(4):
        lane = (iota((128, 2048), 1) & 63) + 64 * (k % 2)
        spread = jnp.where(iota((128, 2048), 0) == lane, 1.0, 0.0).astype(BF16)
        part = ordered[:, 128 * (k // 2) : 128 * (k // 2) + 128]
        wide = jnp.where(own_block, dot(part, spread), 0.0)
        rows.append(jnp.sum(wide, axis=0, keepdims=True))
    return rows


def normed_rows(rows, scale, shift):
    v = rows.astype(F32)
    centre = v - jnp.mean(v, axis=-1, keepdims=True)
    spread = jnp.mean(centre * centre, axis=-1, keepdims=True)
    return (centre * lax.rsqrt(spread + 1e-05) * (1.0 + scale) + shift).astype(BF16)


def unit(v):
    return v * lax.rsqrt(jnp.mean(v * v, axis=-1, keepdims=True) + 1e-06)


def plane_project_kernel(gathered_ref, rows_ref, own_ref, other_ref, q_ref, kv_ref, mod_ref, normed_ref):
    rows = modulation(rows_ref)
    for k in range(4):
        mod_ref[k : k + 1, :] = rows[k]
    for j in range(8):
        normed_ref[16 * j : 16 * j + 16, :] = normed_rows(gathered_ref[j, :, 0:2048], rows[0], rows[1])
    normed = normed_ref[...]
    even = lax.axis_index("zl") == 0
    for i in range(3):
        both = dot(normed, jnp.concatenate([own_ref[i], other_ref[i]], axis=1))
        own, other = both[:, 0:128], both[:, 128:256]
        if i < 2:
            own, other = unit(own), unit(other)
        for h in range(2):
            part = jnp.where(even, own, other) if h == 0 else jnp.where(even, other, own)
            if i == 0:
                q_ref[h] = part.astype(BF16)
            else:
                kv_ref[h, :, 128 * (i - 1) : 128 * i] = part.astype(BF16)


def plane_attend_kernel(scale_ref, q_ref, kv_ref, far_ref, own_ref, other_ref, out_ref):
    even = lax.axis_index("zl") == 0
    y = lax.axis_index("y")
    heads = []
    for h in range(2):
        scale = scale_ref[0, 2 * y + h] / 128.0
        keys = jnp.concatenate([kv_ref[h, :, 0:128], far_ref[h, :, 0:128]], axis=0)
        values = jnp.concatenate([kv_ref[h, :, 128:256], far_ref[h, :, 128:256]], axis=0)
        scores = dot(q_ref[h], keys, ((1,), (1,))) * scale
        expo = jnp.exp(scores - jnp.max(scores, axis=-1, keepdims=True))
        weights = (expo / jnp.sum(expo, axis=-1, keepdims=True)).astype(BF16)
        heads.append(dot(weights, values))
    own = jnp.where(even, heads[0], heads[1])
    other = jnp.where(even, heads[1], heads[0])
    attended = jnp.concatenate([own, other], axis=1).astype(BF16)
    mixing = jnp.concatenate([own_ref[0], other_ref[0]], axis=0)
    for c in range(0, 2048, 512):
        part = dot(attended, mixing[:, c : c + 512]).astype(BF16)
        for j in range(8):
            out_ref[j, :, c : c + 512] = part[16 * j : 16 * j + 16]


def mix_kernel(terms_ref, x_ref, mixed_ref, spread_ref):
    total = terms_ref[0].astype(F32)
    for j in range(1, 8):
        total = total + terms_ref[j].astype(F32)
    mixed = (x_ref[0].astype(F32) + total).astype(BF16)
    mixed_ref[0] = mixed
    for j in range(8):
        spread_ref[j] = mixed


def clock_project_kernel(gathered_ref, mod_ref, own_ref, other_ref, out_ref, normed_ref):
    scale, shift = mod_ref[2:3, :], mod_ref[3:4, :]
    for j in range(8):
        normed_ref[16 * j : 16 * j + 16, :] = normed_rows(gathered_ref[j], scale, shift)
    normed = normed_ref[...]
    even = lax.axis_index("zl") == 0
    upper = iota((16, 8, 128), 1) < 4
    for i in range(3):
        both = dot(normed, jnp.concatenate([own_ref[i], other_ref[i]], axis=1))
        own, other = both[:, 0:128], both[:, 128:256]
        if i < 2:
            own, other = unit(own), unit(other)
        first = jnp.where(even, own, other).reshape(16, 8, 128)
        second = jnp.where(even, other, own).reshape(16, 8, 128)
        low = jnp.where(upper, first, pltpu.roll(second, 4, 1))
        high = jnp.where(upper, pltpu.roll(first, 4, 1), second)
        rows = jnp.stack([low, high], axis=1).reshape(256, 128)
        out_ref[:, 128 * i : 128 * i + 128] = rows.astype(BF16)


def frame_of(index):
    return (index & 24) + (index & 3) * 2 + ((index >> 2) & 1)


def clock_attend_kernel(scale_ref, rows_ref, out_ref):
    y = lax.axis_index("y")
    queries, keys, values = rows_ref[:, 0:128], rows_ref[:, 128:256], rows_ref[:, 256:384]
    r, c = iota((256, 256), 0), iota((256, 256), 1)
    seen = ((r & 7) == (c & 7)) & (frame_of(c >> 3) <= frame_of(r >> 3))
    scale = jnp.where(
        (iota((256, 1), 0) & 7) < 4, scale_ref[1, 2 * y] / 128.0, scale_ref[1, 2 * y + 1] / 128.0
    )
    scores = jnp.where(seen, dot(queries, keys, ((1,), (1,))) * scale, -1e30)
    expo = jnp.exp(scores - jnp.max(scores, axis=-1, keepdims=True))
    weights = (expo / jnp.sum(expo, axis=-1, keepdims=True)).astype(BF16)
    moved = dot(weights, values).reshape(8, 2, 2, 8, 128)
    upper = iota((8, 2, 8, 128), 2) < 4
    even, odd = moved[:, :, 0], moved[:, :, 1]
    first = jnp.where(upper, even, pltpu.roll(odd, 4, 2))
    second = jnp.where(upper, pltpu.roll(even, 4, 2), odd)
    out_ref[...] = jnp.stack([first, second], axis=1).reshape(256, 128).astype(BF16)


def body(x, grades, table, plane_weight, mixing, clock_weight, stretch):
    def shape(*dims, dtype=BF16):
        return jax.ShapeDtypeStruct(dims, dtype)

    def trade(value, axes):
        return lax.all_to_all(value, axes, split_axis=0, concat_axis=0, tiled=True)

    swaps = []
    for z in range(8):
        for core in range(2):
            z_to = (z ^ 1) if core == 0 else (z + 1 if z % 2 else z - 1) % 8
            swaps.append(((z // 2 * 2 + core) * 2 + z % 2, (z_to // 2 * 2 + core) * 2 + z_to % 2))

    def other_head(weight):
        return lax.ppermute(weight, ("zh", "core", "zl"), swaps)

    plane_weight = jnp.transpose(plane_weight, (1, 2, 0, 3)).reshape(3, 2048, 128)
    clock_weight = jnp.transpose(clock_weight, (1, 2, 0, 3)).reshape(3, 2048, 128)
    far_plane = other_head(plane_weight)

    packed = call(
        pack_kernel, shape(8, 16, 2176), grades.reshape(1, -1), jnp.transpose(table, (1, 2, 0)), x
    )
    gathered = trade(packed, "y")
    own_rows = call(frame_rows_kernel, shape(64, 128), gathered)
    mixing, own_rows = lax.optimization_barrier((mixing, own_rows))
    far_mixing = other_head(mixing)
    rows = trade(own_rows, ("zl",) + TM)
    queries, kv, mod = call(
        plane_project_kernel,
        (shape(2, 128, 128), shape(2, 128, 256), shape(8, 2048, dtype=F32)),
        gathered,
        rows,
        plane_weight,
        far_plane,
        flops=2 * 128 * 2048 * 768,
        scratch=[pltpu.VMEM((128, 2048), BF16)],
    )
    terms = call(
        plane_attend_kernel,
        shape(8, 16, 2048),
        stretch,
        queries,
        kv,
        lax.ppermute(kv, "zl", [(0, 1), (1, 0)]),
        mixing,
        far_mixing,
        in_smem=(0,),
        flops=2 * 128 * 2048 * 256,
    )
    clock_weight, terms = lax.optimization_barrier((clock_weight, terms))
    far_clock = other_head(clock_weight)
    mixed, spread = call(mix_kernel, (shape(1, 16, 2048), shape(8, 16, 2048)), trade(terms, "y"), x)
    clock_rows = call(
        clock_project_kernel,
        shape(256, 384),
        trade(spread, "y"),
        mod,
        clock_weight,
        far_clock,
        flops=2 * 128 * 2048 * 768,
        scratch=[pltpu.VMEM((128, 2048), BF16)],
    )
    by_position = trade(clock_rows, ("zh", "core", "x"))
    moved = call(clock_attend_kernel, shape(256, 128), stretch, by_position, in_smem=(0,))
    heads = trade(moved, ("zh", "core", "zl", "x"))
    return mixed, heads.reshape(1, 256, 128)


def solution(mesh):
    named = Mesh(mesh.devices.reshape(4, 4, 2, 8, 2), ("zh", "x", "core", "y", "zl"))
    space = ("y", "zl")
    return jax.shard_map(
        body,
        mesh=named,
        in_specs=(
            P(TM, space, None),
            P(),
            P(None, None, TM + space),
            P(None, None, space, None),
            P(space, None, None),
            P(None, None, space, None),
            P(),
        ),
        out_specs=(P(TM, space, None), P(TM, None, space)),
        check_vma=False,
    )
```

time: 1490 us -> 146 us (0.10)
  blocking collectives: 1250 us -> 73.5 us
  waiting for transfers between devices: 166 us -> 30.1 us
  other arithmetic: 28.7 us -> 0 us
    all_gather x1 -> x0, blocking collectives: 1230 us -> none  [body(): all_levels = lax.all_gather(local_cols, ('tm', 'space'), axis=2, tiled=True)]
    reduce_scatter x1 -> x0, waiting for transfers between devices: 82.3 us -> none  [body(): lax.psum_scatter(jnp.dot(attended, out_weight, preferred_element_type=jnp...]
    all_gather x2 -> x0, waiting for transfers between devices: 71 us -> none  [the longest x1 71 us: body(): lax.all_gather(mixed, 'space', axis=0, tiled=True)]
    all_to_all x1 -> x4, blocking collectives: 14.2 us -> 73.5 us  [trade(): return lax.all_to_all(value, axes, split_axis=0, concat_axis=0, tiled=True)]
    ppermute x0 -> x4, starting transfers between devices: none -> 21.6 us  [the longest x3 19 us: other_head(): return lax.ppermute(weight, ('zh', 'core', 'zl'), swaps)]
    add x1 -> x0, other arithmetic: 17.9 us -> none  [qkv_rows(): 1.0 + scale_row]
  transfers between devices with their start and end apart: 4 -> 6, of which waited for: 3 -> 4; matrix products, arithmetic and copies ran while one was open for 2% -> 0% of each run, Pallas kernels for 0% -> 2%
where the time goes in v1:
time: 146 us; the launch traced here: 145 us
  blocking collectives  73.5 us (50%)
  waiting for transfers between devices  30.1 us (21%)
  starting transfers between devices  28.6 us (20%)
  Pallas kernels  9.02 us (6%)
  local copies, waits for them, and re-layouts  2.94 us (2%)
    all_to_all x4, blocking collectives, trade(): return lax.all_to_all(value, axes, split_axis=0, concat_axis=0, tiled=True)  73.5 us
    all_to_all x2, waiting for transfers between devices, trade(): return lax.all_to_all(value, axes, split_axis=0, concat_axis=0, tiled=True)  24.2 us
    ppermute x3, starting transfers between devices, other_head(): return lax.ppermute(weight, ('zh', 'core', 'zl'), swaps)  19 us
    pallas_call x7, Pallas kernels, call(): pl.pallas_call(kernel, out_shape=out, in_specs=specs, out_specs=outs, scr...  9.02 us
    all_to_all x2, starting transfers between devices, trade(): return lax.all_to_all(value, axes, split_axis=0, concat_axis=0, tiled=True)  6.98 us
    ppermute x1, waiting for transfers between devices, body(): lax.ppermute(kv, 'zl', [(0, 1), (1, 0)])  3.29 us
  transfers between devices with their start and end apart: 6, of which 4 were waited for; matrix products, arithmetic and copies ran while one was open for 0% of the time, Pallas kernels for 2%

profile of v1, /device:TPU:1, one launch (start us, length us, event | category | flops | bytes accessed | tf_op | source)
XLA Modules:
  0.0 144.9 jit_solution(16311131578236220697)
XLA Ops:
  0.6 0.0 copy-start
  0.6 0.0 copy-start.2
  0.7 11.6 %collective-permute-start = (bf16[3,2048,128]{2,1,0:T(8,128)(2,1)}, bf16[3,2048,128]{2,1,0:T(8,128)(2,1)S(1)}, u32[]{:S(2)}, u32[]{:S(2)}) collective-permute-start(bf16[3,2048,128]{2,1,0:T(8,128)(2,1)} %bitcast.20), channel_id=1, source_target_pairs={{0,1},{16,401},{1,0},{17,144},{128,129},{144,17},{129,128},{145,27... | collective-permute-start | bytes 4718600 | tf_op jit(solution)/shard_map/ppermute | solution.py:207
  12.3 0.0 copy-start.3
  12.3 0.8 copy-done.3
  13.1 0.0 copy-start.5
  13.1 0.8 copy-done.5
  13.9 0.0 copy-start.7
  13.9 0.7 copy-done.7
  14.5 0.8 shard_map.86
  15.4 20.1 %all_to_all.46.gathered_ref = bf16[8,16,2176]{2,1,0:T(8,128)(2,1)S(1)} all-to-all(bf16[8,16,2176]{2,1,0:T(8,128)(2,1)S(1)} %shard_map.86), channel_id=1, replica_groups=mesh['zh'=4,'x'=4,'core'=2,'y'=8,'zl'=2] {'y'}, dimensions={0} | all-to-all | bytes 1114112 | tf_op jit(solution)/shard_map/all_to_all | solution.py:198
  35.5 0.1 shard_map.87
  35.6 0.0 copy-done.2
  35.6 4.4 %collective-permute-start.2 = (bf16[1,128,2048]{2,1,0:T(8,128)(2,1)S(1)}, bf16[1,128,2048]{2,1,0:T(8,128)(2,1)S(1)}, u32[]{:S(2)}, u32[]{:S(2)}) collective-permute-start(bf16[1,128,2048]{2,1,0:T(8,128)(2,1)S(1)} %copy-done.2), channel_id=1, source_target_pairs={{0,1},{16,401},{1,0},{17,144},{128,129},{144,17},{129,128},{145,27... | collective-permute-start | bytes 1572872 | tf_op jit(solution)/shard_map/ppermute | solution.py:207
  40.0 19.2 %all_to_all.47 = bf16[64,1,128]{2,1,0:T(2,128)(2,1)S(1)} all-to-all(bf16[64,1,128]{2,1,0:T(2,128)(2,1)S(1)} %copy.15), channel_id=1, replica_groups=mesh['zh'=4,'x'=4,'core'=2,'y'=8,'zl'=2] {'zl','zh','x','core'}, dimensions={0} | all-to-all | bytes 32768 | tf_op jit(solution)/shard_map/all_to_all | solution.py:198
  59.2 0.0 collective-permute-done.other_ref
  59.2 0.0 copy-done
  59.2 0.0 copy-start.6
  59.3 1.3 shard_map.88
  60.6 0.0 copy-start.1
  60.6 0.0 copy-start.4
  60.6 2.5 %collective-permute-start.1 = (bf16[2,128,256]{2,1,0:T(8,128)(2,1)S(1)}, bf16[2,128,256]{2,1,0:T(8,128)(2,1)S(1)}, u32[]{:S(2)}, u32[]{:S(2)}) collective-permute-start(bf16[2,128,256]{2,1,0:T(8,128)(2,1)S(1)} %get-tuple-element.13.kv_ref), channel_id=1, source_target_pairs={{0,1},{1,0},{2,3},{3,2},{4,5},{5,4},{6,7},{7,6},{8,9},{9,8},{10,11... | collective-permute-start | bytes 393224 | tf_op jit(solution)/shard_map/ppermute | solution.py:237
  63.1 0.0 collective-permute-done.2.other_ref
  63.2 3.3 %collective-permute-done.1.far_ref = bf16[2,128,256]{2,1,0:T(8,128)(2,1)S(1)} collective-permute-done((bf16[2,128,256]{2,1,0:T(8,128)(2,1)S(1)}, bf16[2,128,256]{2,1,0:T(8,128)(2,1)S(1)}, u32[]{:S(2)}, u32[]{:S(2)}) %collective-permute-start.1) | collective-permute-done | bytes 131104 | tf_op jit(solution)/shard_map/ppermute | solution.py:237
  66.4 0.0 copy-done.6
  66.4 2.4 %shard_map.89 = bf16[8,16,2048]{2,1,0:T(8,128)(2,1)} custom-call(f32[2,16]{1,0:T(2,128)S(1)} %copy-done.6, bf16[2,128,128]{2,1,0:T(8,128)(2,1)S(1)} %get-tuple-element.12.q_ref, bf16[2,128,256]{2,1,0:T(8,128)(2,1)S(1)} %get-tuple-element.13.kv_ref, bf16[2,128,256]{2,1,0:T(8,128)(2,1)S(1)} %collective-permute-done.1.far_ref, ...), custom_call_target="tpu_custom_call" | custom-call | flops 134217728 | bytes 1376384 | tf_op jit(solution)/shard_map/pallas_call | solution.py:31
  68.9 3.5 %all-to-all-start.2 = ((bf16[8,16,2048]{2,1,0:T(8,128)(2,1)}), bf16[8,16,2048]{2,1,0:T(8,128)(2,1)S(1)}, u32[]{:S(2)}, u32[]{:S(2)}) async-start(bf16[8,16,2048]{2,1,0:T(8,128)(2,1)} %shard_map.89), calls=%async_computation.2 | async-start | bytes 1048576 | tf_op jit(solution)/shard_map/all_to_all | solution.py:198
  72.4 0.0 copy-done.1
  72.4 3.0 %collective-permute-start.3 = (bf16[3,2048,128]{2,1,0:T(8,128)(2,1)S(1)}, bf16[3,2048,128]{2,1,0:T(8,128)(2,1)}, u32[]{:S(2)}, u32[]{:S(2)}) collective-permute-start(bf16[3,2048,128]{2,1,0:T(8,128)(2,1)S(1)} %bitcast.22), channel_id=1, source_target_pairs={{0,1},{16,401},{1,0},{17,144},{128,129},{144,17},{129,128},{145,27... | collective-permute-start | bytes 4718600 | tf_op jit(solution)/shard_map/ppermute | solution.py:207
  75.4 12.4 %all-to-all-done.2.terms_ref = bf16[8,16,2048]{2,1,0:T(8,128)(2,1)S(1)} async-done(((bf16[8,16,2048]{2,1,0:T(8,128)(2,1)}), bf16[8,16,2048]{2,1,0:T(8,128)(2,1)S(1)}, u32[]{:S(2)}, u32[]{:S(2)}) %all-to-all-start.2) | async-done | bytes 524320 | tf_op jit(solution)/shard_map/all_to_all | solution.py:198
  87.8 0.0 copy-done.4
  87.8 0.9 shard_map.90
  88.7 3.5 %all-to-all-start.3 = ((bf16[8,16,2048]{2,1,0:T(8,128)(2,1)}), bf16[8,16,2048]{2,1,0:T(8,128)(2,1)S(1)}, u32[]{:S(2)}, u32[]{:S(2)}) async-start(bf16[8,16,2048]{2,1,0:T(8,128)(2,1)} %get-tuple-element.17), calls=%async_computation.3 | async-start | bytes 1048576 | tf_op jit(solution)/shard_map/all_to_all | solution.py:198
  92.2 2.6 %collective-permute-done.3.other_ref = bf16[3,2048,128]{2,1,0:T(8,128)(2,1)} collective-permute-done((bf16[3,2048,128]{2,1,0:T(8,128)(2,1)S(1)}, bf16[3,2048,128]{2,1,0:T(8,128)(2,1)}, u32[]{:S(2)}, u32[]{:S(2)}) %collective-permute-start.3) | collective-permute-done | bytes 1572896 | tf_op jit(solution)/shard_map/ppermute | solution.py:207
  94.8 11.8 %all-to-all-done.3.gathered_ref = bf16[8,16,2048]{2,1,0:T(8,128)(2,1)S(1)} async-done(((bf16[8,16,2048]{2,1,0:T(8,128)(2,1)}), bf16[8,16,2048]{2,1,0:T(8,128)(2,1)S(1)}, u32[]{:S(2)}, u32[]{:S(2)}) %all-to-all-start.3) | async-done | bytes 524320 | tf_op jit(solution)/shard_map/all_to_all | solution.py:198
  106.6 2.4 %shard_map.91 = bf16[256,384]{1,0:T(8,128)(2,1)S(1)} custom-call(bf16[8,16,2048]{2,1,0:T(8,128)(2,1)S(1)} %all-to-all-done.3.gathered_ref, f32[8,2048]{1,0:T(8,128)S(1)} %get-tuple-element.18.mod_ref, bf16[3,2048,128]{2,1,0:T(8,128)(2,1)S(1)} %bitcast.23, bf16[3,2048,128]{2,1,0:T(8,128)(2,1)} %collective-permute-done.3.other_ref), custom_call_target="tpu_custom_call" | custom-call | flops 402653184 | bytes 3735552 | tf_op jit(solution)/shard_map/pallas_call | solution.py:31
  109.0 20.6 %all_to_all.48 = bf16[32,8,384]{2,1,0:T(8,128)(2,1)S(1)} all-to-all(bf16[32,8,384]{2,1,0:T(8,128)(2,1)S(1)} %bitcast.25), channel_id=1, replica_groups=mesh['zh'=4,'x'=4,'core'=2,'y'=8,'zl'=2] {'zh','core','x'}, dimensions={0} | all-to-all | bytes 393216 | tf_op jit(solution)/shard_map/all_to_all | solution.py:198
  129.6 1.1 shard_map.92
  130.7 13.6 %all_to_all.49 = bf16[64,4,128]{2,1,0:T(4,128)(2,1)S(1)} all-to-all(bf16[64,4,128]{2,1,0:T(4,128)(2,1)S(1)} %bitcast.26), channel_id=1, replica_groups=mesh['zh'=4,'x'=4,'core'=2,'y'=8,'zl'=2] {'zh','core','zl','x'}, dimensions={0} | all-to-all | bytes 131072 | tf_op jit(solution)/shard_map/all_to_all | solution.py:198
  144.3 0.6 copy.21
  (2 shorter events, 0.0 us)
Async XLA Ops:
  0.6 58.6 %copy-start = (bf16[2048,3,1,128]{3,0,2,1:T(8,128)(2,1)S(1)}, bf16[2048,3,1,128]{3,0,2,1:T(8,128)(2,1)}, u32[]{:S(2)}) copy-start(bf16[2048,3,1,128]{3,0,2,1:T(8,128)(2,1)} %param.10) | copy-start | bytes 4718596
  0.6 34.9 %copy-start.2 = (bf16[1,128,2048]{2,1,0:T(8,128)(2,1)S(1)}, bf16[1,128,2048]{2,1,0:T(8,128)(2,1)}, u32[]{:S(2)}) copy-start(bf16[1,128,2048]{2,1,0:T(8,128)(2,1)} %own_ref) | copy-start | bytes 1572868
  0.7 58.6 %collective-permute-start = (bf16[3,2048,128]{2,1,0:T(8,128)(2,1)}, bf16[3,2048,128]{2,1,0:T(8,128)(2,1)S(1)}, u32[]{:S(2)}, u32[]{:S(2)}) collective-permute-start(bf16[3,2048,128]{2,1,0:T(8,128)(2,1)} %bitcast.20), channel_id=1, source_target_pairs={{0,1},{16,401},{1,0},{17,144},{128,129},{144,17},{129,128},{145,27... | collective-permute-start | bytes 4718600 | tf_op jit(solution)/shard_map/ppermute | solution.py:207
  12.3 0.8 copy-start.3
  13.1 0.8 copy-start.5
  13.9 0.7 copy-start.7
  35.6 27.6 %collective-permute-start.2 = (bf16[1,128,2048]{2,1,0:T(8,128)(2,1)S(1)}, bf16[1,128,2048]{2,1,0:T(8,128)(2,1)S(1)}, u32[]{:S(2)}, u32[]{:S(2)}) collective-permute-start(bf16[1,128,2048]{2,1,0:T(8,128)(2,1)S(1)} %copy-done.2), channel_id=1, source_target_pairs={{0,1},{16,401},{1,0},{17,144},{128,129},{144,17},{129,128},{145,27... | collective-permute-start | bytes 1572872 | tf_op jit(solution)/shard_map/ppermute | solution.py:207
  59.2 7.2 %copy-start.6 = (f32[2,16]{1,0:T(2,128)S(1)}, f32[2,16]{1,0:T(2,128)}, u32[]{:S(2)}) copy-start(f32[2,16]{1,0:T(2,128)} %scale_ref.3) | copy-start | bytes 388
  60.6 11.8 %copy-start.1 = (bf16[2048,3,1,128]{3,0,2,1:T(8,128)(2,1)S(1)}, bf16[2048,3,1,128]{3,0,2,1:T(8,128)(2,1)}, u32[]{:S(2)}) copy-start(bf16[2048,3,1,128]{3,0,2,1:T(8,128)(2,1)} %param.12) | copy-start | bytes 4718596
  60.6 27.2 %copy-start.4 = (bf16[1,16,2048]{2,1,0:T(8,128)(2,1)S(1)}, bf16[1,16,2048]{2,1,0:T(8,128)(2,1)}, u32[]{:S(2)}) copy-start(bf16[1,16,2048]{2,1,0:T(8,128)(2,1)} %x_ref.3) | copy-start | bytes 196612
  60.6 5.8 %collective-permute-start.1 = (bf16[2,128,256]{2,1,0:T(8,128)(2,1)S(1)}, bf16[2,128,256]{2,1,0:T(8,128)(2,1)S(1)}, u32[]{:S(2)}, u32[]{:S(2)}) collective-permute-start(bf16[2,128,256]{2,1,0:T(8,128)(2,1)S(1)} %get-tuple-element.13.kv_ref), channel_id=1, source_target_pairs={{0,1},{1,0},{2,3},{3,2},{4,5},{5,4},{6,7},{7,6},{8,9},{9,8},{10,11... | collective-permute-start | bytes 393224 | tf_op jit(solution)/shard_map/ppermute | solution.py:237
  68.9 18.9 %all-to-all-start.2 = ((bf16[8,16,2048]{2,1,0:T(8,128)(2,1)}), bf16[8,16,2048]{2,1,0:T(8,128)(2,1)S(1)}, u32[]{:S(2)}, u32[]{:S(2)}) async-start(bf16[8,16,2048]{2,1,0:T(8,128)(2,1)} %shard_map.89), calls=%async_computation.2 | async-start | bytes 1048576 | tf_op jit(solution)/shard_map/all_to_all | solution.py:198
  72.4 22.5 %collective-permute-start.3 = (bf16[3,2048,128]{2,1,0:T(8,128)(2,1)S(1)}, bf16[3,2048,128]{2,1,0:T(8,128)(2,1)}, u32[]{:S(2)}, u32[]{:S(2)}) collective-permute-start(bf16[3,2048,128]{2,1,0:T(8,128)(2,1)S(1)} %bitcast.22), channel_id=1, source_target_pairs={{0,1},{16,401},{1,0},{17,144},{128,129},{144,17},{129,128},{145,27... | collective-permute-start | bytes 4718600 | tf_op jit(solution)/shard_map/ppermute | solution.py:207
  88.7 17.9 %all-to-all-start.3 = ((bf16[8,16,2048]{2,1,0:T(8,128)(2,1)}), bf16[8,16,2048]{2,1,0:T(8,128)(2,1)S(1)}, u32[]{:S(2)}, u32[]{:S(2)}) async-start(bf16[8,16,2048]{2,1,0:T(8,128)(2,1)} %get-tuple-element.17), calls=%async_computation.3 | async-start | bytes 1048576 | tf_op jit(solution)/shard_map/all_to_all | solution.py:198

commit v2 on v1

--- a/solution.py
+++ b/solution.py
@@ -9,7 +9,7 @@
 from jax.sharding import PartitionSpec as P
 
 TM = ("zh", "x", "core")
-VMEM_LIMIT = 48 * 1024 * 1024
+VMEM_LIMIT = 16 * 1024 * 1024
 BF16 = jnp.bfloat16
 F32 = jnp.float32
 
@@ -115,14 +115,14 @@
                 kv_ref[h, :, 128 * (i - 1) : 128 * i] = part.astype(BF16)
 
 
-def plane_attend_kernel(scale_ref, q_ref, kv_ref, far_ref, own_ref, other_ref, out_ref):
+def plane_attend_kernel(scale_ref, q_ref, kv_ref, own_ref, other_ref, out_ref):
     even = lax.axis_index("zl") == 0
     y = lax.axis_index("y")
     heads = []
     for h in range(2):
         scale = scale_ref[0, 2 * y + h] / 128.0
-        keys = jnp.concatenate([kv_ref[h, :, 0:128], far_ref[h, :, 0:128]], axis=0)
-        values = jnp.concatenate([kv_ref[h, :, 128:256], far_ref[h, :, 128:256]], axis=0)
+        keys = jnp.concatenate([kv_ref[0, h, :, 0:128], kv_ref[1, h, :, 0:128]], axis=0)
+        values = jnp.concatenate([kv_ref[0, h, :, 128:256], kv_ref[1, h, :, 128:256]], axis=0)
         scores = dot(q_ref[h], keys, ((1,), (1,))) * scale
         expo = jnp.exp(scores - jnp.max(scores, axis=-1, keepdims=True))
         weights = (expo / jnp.sum(expo, axis=-1, keepdims=True)).astype(BF16)
@@ -208,15 +208,14 @@
 
     plane_weight = jnp.transpose(plane_weight, (1, 2, 0, 3)).reshape(3, 2048, 128)
     clock_weight = jnp.transpose(clock_weight, (1, 2, 0, 3)).reshape(3, 2048, 128)
-    far_plane = other_head(plane_weight)
-
     packed = call(
         pack_kernel, shape(8, 16, 2176), grades.reshape(1, -1), jnp.transpose(table, (1, 2, 0)), x
     )
+    far_plane = other_head(plane_weight)
+    packed, mixing = lax.optimization_barrier((packed, mixing))
+    far_mixing = other_head(mixing)
     gathered = trade(packed, "y")
     own_rows = call(frame_rows_kernel, shape(64, 128), gathered)
-    mixing, own_rows = lax.optimization_barrier((mixing, own_rows))
-    far_mixing = other_head(mixing)
     rows = trade(own_rows, ("zl",) + TM)
     queries, kv, mod = call(
         plane_project_kernel,
@@ -233,8 +232,7 @@
         shape(8, 16, 2048),
         stretch,
         queries,
-        kv,
-        lax.ppermute(kv, "zl", [(0, 1), (1, 0)]),
+        lax.all_gather(kv, "zl"),
         mixing,
         far_mixing,
         in_smem=(0,),

time: 146 us -> 143 us (0.979)
  blocking collectives: 73.5 us -> 59 us
  waiting for transfers between devices: 30.1 us -> 38.4 us
  Pallas kernels: 9.02 us -> 11.3 us
  starting transfers between devices: 28.6 us -> 30.4 us
    all_to_all x4 -> x3, blocking collectives: 73.5 us -> 54.5 us  [trade(): return lax.all_to_all(value, axes, split_axis=0, concat_axis=0, tiled=True)]
    all_to_all x2 -> x3, waiting for transfers between devices: 24.2 us -> 35.7 us  [trade(): return lax.all_to_all(value, axes, split_axis=0, concat_axis=0, tiled=True)]
    all_to_all x2 -> x3, starting transfers between devices: 6.98 us -> 13.8 us  [trade(): return lax.all_to_all(value, axes, split_axis=0, concat_axis=0, tiled=True)]
    all_gather x0 -> x1, blocking collectives: none -> 4.5 us  [body(): lax.all_gather(kv, 'zl')]
    ppermute x1 -> x0, waiting for transfers between devices: 3.29 us -> none  [body(): lax.ppermute(kv, 'zl', [(0, 1), (1, 0)])]
    ppermute x1 -> x0, starting transfers between devices: 2.54 us -> none  [body(): lax.ppermute(kv, 'zl', [(0, 1), (1, 0)])]
    ppermute x3, starting transfers between devices: 19 us -> 16.6 us  [other_head(): return lax.ppermute(weight, ('zh', 'core', 'zl'), swaps)]
    pallas_call x7, Pallas kernels: 9.02 us -> 11.3 us  [call(): pl.pallas_call(kernel, out_shape=out, in_specs=specs, out_specs=outs, scr...]
  transfers between devices with their start and end apart: 6 -> 6, of which waited for: 4 -> 4; matrix products, arithmetic and copies ran while one was open for 0% -> 0% of each run, Pallas kernels for 2% -> 4%
where the time goes in v2:
time: 143 us
  blocking collectives  59 us (41%)
  waiting for transfers between devices  38.4 us (27%)
  starting transfers between devices  30.4 us (21%)
  Pallas kernels  11.3 us (8%)
  local copies, waits for them, and re-layouts  2.93 us (2%)
    all_to_all x3, blocking collectives, trade(): return lax.all_to_all(value, axes, split_axis=0, concat_axis=0, tiled=True)  54.5 us
    all_to_all x3, waiting for transfers between devices, trade(): return lax.all_to_all(value, axes, split_axis=0, concat_axis=0, tiled=True)  35.7 us
    ppermute x3, starting transfers between devices, other_head(): return lax.ppermute(weight, ('zh', 'core', 'zl'), swaps)  16.6 us
    all_to_all x3, starting transfers between devices, trade(): return lax.all_to_all(value, axes, split_axis=0, concat_axis=0, tiled=True)  13.8 us
    pallas_call x7, Pallas kernels, call(): pl.pallas_call(kernel, out_shape=out, in_specs=specs, out_specs=outs, scr...  11.3 us
    all_gather x1, blocking collectives, body(): lax.all_gather(kv, 'zl')  4.5 us
    unnamed x18, local copies, waits for them, and re-layouts  2.91 us
  transfers between devices with their start and end apart: 6, of which 4 were waited for; matrix products, arithmetic and copies ran while one was open for 0% of the time, Pallas kernels for 4%

profile of v2, /device:TPU:1, one launch (start us, length us, event | category | flops | bytes accessed | tf_op | source)
XLA Modules:
  0.0 142.7 jit_solution(9997894563739733471)
XLA Ops:
  0.6 0.0 copy-start
  0.6 11.6 %collective-permute-start = (bf16[3,2048,128]{2,1,0:T(8,128)(2,1)}, bf16[3,2048,128]{2,1,0:T(8,128)(2,1)}, u32[]{:S(2)}, u32[]{:S(2)}) collective-permute-start(bf16[3,2048,128]{2,1,0:T(8,128)(2,1)} %bitcast.21), channel_id=1, source_target_pairs={{0,1},{16,401},{1,0},{17,144},{128,129},{144,17},{129,128},{145,27... | collective-permute-start | bytes 4718600 | tf_op jit(solution)/shard_map/ppermute | solution.py:207
  12.3 0.0 copy-start.3
  12.3 0.8 copy-done.3
  13.1 0.0 copy-start.5
  13.1 0.8 copy-done.5
  13.9 0.0 copy-start.7
  13.9 0.7 copy-done.7
  14.5 1.7 %shard_map.86 = bf16[8,16,2176]{2,1,0:T(8,128)(2,1)} custom-call(s32[1,32]{1,0:T(1,128)S(1)} %bitcast.32, bf16[4,4,1000]{2,1,0:T(4,128)(2,1)S(1)} %bitcast.31, bf16[1,16,2048]{2,1,0:T(8,128)(2,1)S(1)} %copy-done.3), custom_call_target="tpu_custom_call" | custom-call | bytes 97664 | tf_op jit(solution)/shard_map/pallas_call | solution.py:31
  16.2 6.8 %all-to-all-start = ((bf16[8,16,2176]{2,1,0:T(8,128)(2,1)}), bf16[8,16,2176]{2,1,0:T(8,128)(2,1)S(1)}, u32[]{:S(2)}, u32[]{:S(2)}) async-start(bf16[8,16,2176]{2,1,0:T(8,128)(2,1)} %shard_map.86), calls=%async_computation | async-start | bytes 1114112 | tf_op jit(solution)/shard_map/all_to_all | solution.py:198
  23.0 1.9 %collective-permute-start.1 = (bf16[1,128,2048]{2,1,0:T(8,128)(2,1)}, bf16[1,128,2048]{2,1,0:T(8,128)(2,1)S(1)}, u32[]{:S(2)}, u32[]{:S(2)}) collective-permute-start(bf16[1,128,2048]{2,1,0:T(8,128)(2,1)} %own_ref), channel_id=1, source_target_pairs={{0,1},{16,401},{1,0},{17,144},{128,129},{144,17},{129,128},{145,27... | collective-permute-start | bytes 1572872 | tf_op jit(solution)/shard_map/ppermute | solution.py:207
  24.9 11.6 %all-to-all-done.gathered_ref = bf16[8,16,2176]{2,1,0:T(8,128)(2,1)S(1)} async-done(((bf16[8,16,2176]{2,1,0:T(8,128)(2,1)}), bf16[8,16,2176]{2,1,0:T(8,128)(2,1)S(1)}, u32[]{:S(2)}, u32[]{:S(2)}) %all-to-all-start) | async-done | bytes 557088 | tf_op jit(solution)/shard_map/all_to_all | solution.py:198
  36.5 0.1 shard_map.87
  36.6 20.3 %all_to_all.46 = bf16[64,1,128]{2,1,0:T(2,128)(2,1)S(1)} all-to-all(bf16[64,1,128]{2,1,0:T(2,128)(2,1)S(1)} %copy.15), channel_id=1, replica_groups=mesh['zh'=4,'x'=4,'core'=2,'y'=8,'zl'=2] {'zl','zh','x','core'}, dimensions={0} | all-to-all | bytes 32768 | tf_op jit(solution)/shard_map/all_to_all | solution.py:198
  56.9 0.0 collective-permute-done.other_ref
  56.9 0.0 copy-done
  56.9 0.0 copy-start.2
  57.0 0.0 copy-start.6
  57.0 2.8 %shard_map.88 = (bf16[2,128,128]{2,1,0:T(8,128)(2,1)S(1)}, bf16[2,128,256]{2,1,0:T(8,128)(2,1)S(1)}, f32[8,2048]{1,0:T(8,128)S(1)}) custom-call(bf16[8,16,2176]{2,1,0:T(8,128)(2,1)S(1)} %all-to-all-done.gathered_ref, bf16[64,128]{1,0:T(8,128)(2,1)S(1)} %bitcast.29, bf16[3,2048,128]{2,1,0:T(8,128)(2,1)S(1)} %bitcast.22, ...), custom_call_target="tpu_custom_call" | custom-call | flops 402653184 | bytes 3719168 | tf_op jit(solution)/shard_map/pallas_call | solution.py:31
  59.8 4.5 %all-gather = bf16[4,128,256]{2,1,0:T(8,128)(2,1)S(1)} all-gather(bf16[2,128,256]{2,1,0:T(8,128)(2,1)S(1)} %get-tuple-element.13), channel_id=2, replica_groups=mesh['zh'=4,'x'=4,'core'=2,'y'=8,'zl'=2] {'zl'}, dimensions={0}, use_global_device_ids=true | all-gather | bytes 393216 | tf_op jit(solution)/shard_map/all_gather | solution.py:235
  64.3 0.0 copy-start.1
  64.3 0.0 copy-start.4
  64.3 0.0 collective-permute-done.1.other_ref
  64.3 0.0 copy-done.2
  64.3 0.0 copy-done.6
  64.3 2.4 %shard_map.89 = bf16[8,16,2048]{2,1,0:T(8,128)(2,1)} custom-call(f32[2,16]{1,0:T(2,128)S(1)} %copy-done.6, bf16[2,128,128]{2,1,0:T(8,128)(2,1)S(1)} %get-tuple-element.12.q_ref, bf16[2,2,128,256]{3,2,1,0:T(8,128)(2,1)S(1)} %bitcast.25, bf16[1,128,2048]{2,1,0:T(8,128)(2,1)S(1)} %copy-done.2, bf16[1,128,2048]{2,1,0:T(8,128)(2,1)S(1)} %collective-permute-done.1.other_ref), custom_call_target="tpu_custom_call" | custom-call | flops 134217728 | bytes 1376384 | tf_op jit(solution)/shard_map/pallas_call | solution.py:31
  66.7 3.5 %all-to-all-start.2 = ((bf16[8,16,2048]{2,1,0:T(8,128)(2,1)}), bf16[8,16,2048]{2,1,0:T(8,128)(2,1)S(1)}, u32[]{:S(2)}, u32[]{:S(2)}) async-start(bf16[8,16,2048]{2,1,0:T(8,128)(2,1)} %shard_map.89), calls=%async_computation.2 | async-start | bytes 1048576 | tf_op jit(solution)/shard_map/all_to_all | solution.py:198
  70.2 0.0 copy-done.1
  70.2 3.0 %collective-permute-start.2 = (bf16[3,2048,128]{2,1,0:T(8,128)(2,1)S(1)}, bf16[3,2048,128]{2,1,0:T(8,128)(2,1)}, u32[]{:S(2)}, u32[]{:S(2)}) collective-permute-start(bf16[3,2048,128]{2,1,0:T(8,128)(2,1)S(1)} %bitcast.23), channel_id=1, source_target_pairs={{0,1},{16,401},{1,0},{17,144},{128,129},{144,17},{129,128},{145,27... | collective-permute-start | bytes 4718600 | tf_op jit(solution)/shard_map/ppermute | solution.py:207
  73.2 12.4 %all-to-all-done.2.terms_ref = bf16[8,16,2048]{2,1,0:T(8,128)(2,1)S(1)} async-done(((bf16[8,16,2048]{2,1,0:T(8,128)(2,1)}), bf16[8,16,2048]{2,1,0:T(8,128)(2,1)S(1)}, u32[]{:S(2)}, u32[]{:S(2)}) %all-to-all-start.2) | async-done | bytes 524320 | tf_op jit(solution)/shard_map/all_to_all | solution.py:198
  85.6 0.0 copy-done.4
  85.6 0.9 shard_map.90
  86.6 3.5 %all-to-all-start.3 = ((bf16[8,16,2048]{2,1,0:T(8,128)(2,1)}), bf16[8,16,2048]{2,1,0:T(8,128)(2,1)S(1)}, u32[]{:S(2)}, u32[]{:S(2)}) async-start(bf16[8,16,2048]{2,1,0:T(8,128)(2,1)} %get-tuple-element.17), calls=%async_computation.3 | async-start | bytes 1048576 | tf_op jit(solution)/shard_map/all_to_all | solution.py:198
  90.1 2.6 %collective-permute-done.2.other_ref = bf16[3,2048,128]{2,1,0:T(8,128)(2,1)} collective-permute-done((bf16[3,2048,128]{2,1,0:T(8,128)(2,1)S(1)}, bf16[3,2048,128]{2,1,0:T(8,128)(2,1)}, u32[]{:S(2)}, u32[]{:S(2)}) %collective-permute-start.2) | collective-permute-done | bytes 1572896 | tf_op jit(solution)/shard_map/ppermute | solution.py:207
  92.7 11.8 %all-to-all-done.3.gathered_ref = bf16[8,16,2048]{2,1,0:T(8,128)(2,1)S(1)} async-done(((bf16[8,16,2048]{2,1,0:T(8,128)(2,1)}), bf16[8,16,2048]{2,1,0:T(8,128)(2,1)S(1)}, u32[]{:S(2)}, u32[]{:S(2)}) %all-to-all-start.3) | async-done | bytes 524320 | tf_op jit(solution)/shard_map/all_to_all | solution.py:198
  104.5 2.4 %shard_map.91 = bf16[256,384]{1,0:T(8,128)(2,1)S(1)} custom-call(bf16[8,16,2048]{2,1,0:T(8,128)(2,1)S(1)} %all-to-all-done.3.gathered_ref, f32[8,2048]{1,0:T(8,128)S(1)} %get-tuple-element.18.mod_ref, bf16[3,2048,128]{2,1,0:T(8,128)(2,1)S(1)} %bitcast.24, bf16[3,2048,128]{2,1,0:T(8,128)(2,1)} %collective-permute-done.2.other_ref), custom_call_target="tpu_custom_call" | custom-call | flops 402653184 | bytes 3735552 | tf_op jit(solution)/shard_map/pallas_call | solution.py:31
  106.8 20.6 %all_to_all.47 = bf16[32,8,384]{2,1,0:T(8,128)(2,1)S(1)} all-to-all(bf16[32,8,384]{2,1,0:T(8,128)(2,1)S(1)} %bitcast.27), channel_id=1, replica_groups=mesh['zh'=4,'x'=4,'core'=2,'y'=8,'zl'=2] {'zh','core','x'}, dimensions={0} | all-to-all | bytes 393216 | tf_op jit(solution)/shard_map/all_to_all | solution.py:198
  127.5 1.1 shard_map.92
  128.5 13.6 %all_to_all.48 = bf16[64,4,128]{2,1,0:T(4,128)(2,1)S(1)} all-to-all(bf16[64,4,128]{2,1,0:T(4,128)(2,1)S(1)} %bitcast.28), channel_id=1, replica_groups=mesh['zh'=4,'x'=4,'core'=2,'y'=8,'zl'=2] {'zh','core','zl','x'}, dimensions={0} | all-to-all | bytes 131072 | tf_op jit(solution)/shard_map/all_to_all | solution.py:198
  142.1 0.6 copy.21
  (2 shorter events, 0.0 us)
Async XLA Ops:
  0.6 56.3 %copy-start = (bf16[2048,3,1,128]{3,0,2,1:T(8,128)(2,1)S(1)}, bf16[2048,3,1,128]{3,0,2,1:T(8,128)(2,1)}, u32[]{:S(2)}) copy-start(bf16[2048,3,1,128]{3,0,2,1:T(8,128)(2,1)} %param.10) | copy-start | bytes 4718596
  0.6 56.3 %collective-permute-start = (bf16[3,2048,128]{2,1,0:T(8,128)(2,1)}, bf16[3,2048,128]{2,1,0:T(8,128)(2,1)}, u32[]{:S(2)}, u32[]{:S(2)}) collective-permute-start(bf16[3,2048,128]{2,1,0:T(8,128)(2,1)} %bitcast.21), channel_id=1, source_target_pairs={{0,1},{16,401},{1,0},{17,144},{128,129},{144,17},{129,128},{145,27... | collective-permute-start | bytes 4718600 | tf_op jit(solution)/shard_map/ppermute | solution.py:207
  12.3 0.8 copy-start.3
  13.1 0.8 copy-start.5
  13.9 0.7 copy-start.7
  16.2 20.3 %all-to-all-start = ((bf16[8,16,2176]{2,1,0:T(8,128)(2,1)}), bf16[8,16,2176]{2,1,0:T(8,128)(2,1)S(1)}, u32[]{:S(2)}, u32[]{:S(2)}) async-start(bf16[8,16,2176]{2,1,0:T(8,128)(2,1)} %shard_map.86), calls=%async_computation | async-start | bytes 1114112 | tf_op jit(solution)/shard_map/all_to_all | solution.py:198
  23.0 41.3 %collective-permute-start.1 = (bf16[1,128,2048]{2,1,0:T(8,128)(2,1)}, bf16[1,128,2048]{2,1,0:T(8,128)(2,1)S(1)}, u32[]{:S(2)}, u32[]{:S(2)}) collective-permute-start(bf16[1,128,2048]{2,1,0:T(8,128)(2,1)} %own_ref), channel_id=1, source_target_pairs={{0,1},{16,401},{1,0},{17,144},{128,129},{144,17},{129,128},{145,27... | collective-permute-start | bytes 1572872 | tf_op jit(solution)/shard_map/ppermute | solution.py:207
  56.9 7.3 %copy-start.2 = (bf16[1,128,2048]{2,1,0:T(8,128)(2,1)S(1)}, bf16[1,128,2048]{2,1,0:T(8,128)(2,1)}, u32[]{:S(2)}) copy-start(bf16[1,128,2048]{2,1,0:T(8,128)(2,1)} %own_ref) | copy-start | bytes 1572868
  57.0 7.3 %copy-start.6 = (f32[2,16]{1,0:T(2,128)S(1)}, f32[2,16]{1,0:T(2,128)}, u32[]{:S(2)}) copy-start(f32[2,16]{1,0:T(2,128)} %scale_ref.3) | copy-start | bytes 388
  64.3 5.9 %copy-start.1 = (bf16[2048,3,1,128]{3,0,2,1:T(8,128)(2,1)S(1)}, bf16[2048,3,1,128]{3,0,2,1:T(8,128)(2,1)}, u32[]{:S(2)}) copy-start(bf16[2048,3,1,128]{3,0,2,1:T(8,128)(2,1)} %param.12) | copy-start | bytes 4718596
  64.3 21.4 %copy-start.4 = (bf16[1,16,2048]{2,1,0:T(8,128)(2,1)S(1)}, bf16[1,16,2048]{2,1,0:T(8,128)(2,1)}, u32[]{:S(2)}) copy-start(bf16[1,16,2048]{2,1,0:T(8,128)(2,1)} %x_ref.3) | copy-start | bytes 196612
  66.7 18.9 %all-to-all-start.2 = ((bf16[8,16,2048]{2,1,0:T(8,128)(2,1)}), bf16[8,16,2048]{2,1,0:T(8,128)(2,1)S(1)}, u32[]{:S(2)}, u32[]{:S(2)}) async-start(bf16[8,16,2048]{2,1,0:T(8,128)(2,1)} %shard_map.89), calls=%async_computation.2 | async-start | bytes 1048576 | tf_op jit(solution)/shard_map/all_to_all | solution.py:198
  70.2 22.5 %collective-permute-start.2 = (bf16[3,2048,128]{2,1,0:T(8,128)(2,1)S(1)}, bf16[3,2048,128]{2,1,0:T(8,128)(2,1)}, u32[]{:S(2)}, u32[]{:S(2)}) collective-permute-start(bf16[3,2048,128]{2,1,0:T(8,128)(2,1)S(1)} %bitcast.23), channel_id=1, source_target_pairs={{0,1},{16,401},{1,0},{17,144},{128,129},{144,17},{129,128},{145,27... | collective-permute-start | bytes 4718600 | tf_op jit(solution)/shard_map/ppermute | solution.py:207
  86.6 17.9 %all-to-all-start.3 = ((bf16[8,16,2048]{2,1,0:T(8,128)(2,1)}), bf16[8,16,2048]{2,1,0:T(8,128)(2,1)S(1)}, u32[]{:S(2)}, u32[]{:S(2)}) async-start(bf16[8,16,2048]{2,1,0:T(8,128)(2,1)} %get-tuple-element.17), calls=%async_computation.3 | async-start | bytes 1048576 | tf_op jit(solution)/shard_map/all_to_all | solution.py:198

commit v3 on v2

--- a/solution.py
+++ b/solution.py
@@ -22,10 +22,11 @@
     return lax.dot_general(a, b, (dims, ((), ())), preferred_element_type=F32)
 
 
-def call(kernel, out, *args, in_smem=(), flops=0, scratch=()):
-    specs = [
-        pl.BlockSpec(memory_space=pltpu.SMEM if i in in_smem else pltpu.VMEM) for i in range(len(args))
-    ]
+def call(kernel, out, *args, in_smem=(), anywhere=(), flops=0, scratch=()):
+    def space(i):
+        return pltpu.SMEM if i in in_smem else pl.ANY if i in anywhere else pltpu.VMEM
+
+    specs = [pl.BlockSpec(memory_space=space(i)) for i in range(len(args))]
     outs = jax.tree.map(lambda _: pl.BlockSpec(memory_space=pltpu.VMEM), out)
     total = sum(a.size * a.dtype.itemsize for a in args)
     return pl.pallas_call(
@@ -94,7 +95,11 @@
     return v * lax.rsqrt(jnp.mean(v * v, axis=-1, keepdims=True) + 1e-06)
 
 
-def plane_project_kernel(gathered_ref, rows_ref, own_ref, other_ref, q_ref, kv_ref, mod_ref, normed_ref):
+def plane_project_kernel(
+    gathered_ref, rows_ref, own_ref, other_ref, other_any, q_ref, kv_ref, mod_ref, normed_ref, last_ref, sem
+):
+    copy = pltpu.make_async_copy(other_any.at[2], last_ref, sem)
+    copy.start()
     rows = modulation(rows_ref)
     for k in range(4):
         mod_ref[k : k + 1, :] = rows[k]
@@ -103,7 +108,9 @@
     normed = normed_ref[...]
     even = lax.axis_index("zl") == 0
     for i in range(3):
-        both = dot(normed, jnp.concatenate([own_ref[i], other_ref[i]], axis=1))
+        if i == 2:
+            copy.wait()
+        both = dot(normed, jnp.concatenate([own_ref[i], last_ref[...] if i == 2 else other_ref[i]], axis=1))
         own, other = both[:, 0:128], both[:, 128:256]
         if i < 2:
             own, other = unit(own), unit(other)
@@ -137,6 +144,23 @@
             out_ref[j, :, c : c + 512] = part[16 * j : 16 * j + 16]
 
 
+def hold_kernel(weight_ref, out_ref):
+    out_ref[...] = weight_ref[...]
+
+
+def hold(weight):
+    block = (2,) + weight.shape[1:]
+    return pl.pallas_call(
+        hold_kernel,
+        grid=(1,),
+        out_shape=jax.ShapeDtypeStruct(block, weight.dtype),
+        in_specs=[pl.BlockSpec(block, lambda i: (0, 0, 0))],
+        out_specs=pl.BlockSpec(block, lambda i: (0, 0, 0)),
+        compiler_params=pltpu.CompilerParams(vmem_limit_bytes=VMEM_LIMIT),
+        cost_estimate=pl.CostEstimate(flops=0, bytes_accessed=2**22, transcendentals=0),
+    )(weight)
+
+
 def mix_kernel(terms_ref, x_ref, mixed_ref, spread_ref):
     total = terms_ref[0].astype(F32)
     for j in range(1, 8):
@@ -203,6 +227,12 @@
             z_to = (z ^ 1) if core == 0 else (z + 1 if z % 2 else z - 1) % 8
             swaps.append(((z // 2 * 2 + core) * 2 + z % 2, (z_to // 2 * 2 + core) * 2 + z_to % 2))
 
+    project_scratch = [
+        pltpu.VMEM((128, 2048), BF16),
+        pltpu.VMEM((2048, 128), BF16),
+        pltpu.SemaphoreType.DMA,
+    ]
+
     def other_head(weight):
         return lax.ppermute(weight, ("zh", "core", "zl"), swaps)
 
@@ -223,9 +253,11 @@
         gathered,
         rows,
         plane_weight,
+        hold(far_plane),
         far_plane,
+        anywhere=(4,),
         flops=2 * 128 * 2048 * 768,
-        scratch=[pltpu.VMEM((128, 2048), BF16)],
+        scratch=project_scratch,
     )
     terms = call(
         plane_attend_kernel,

time: 143 us -> 143 us (level)
  transfers between devices with their start and end apart: 6 -> 6, of which waited for: 4 -> 4; matrix products, arithmetic and copies ran while one was open for 0% -> 0% of each run, Pallas kernels for 4% -> 3%
where the time goes in v3:
time: 143 us; the launch traced here: 142 us
  blocking collectives  59.1 us (41%)
  waiting for transfers between devices  38.3 us (27%)
  starting transfers between devices  30.4 us (21%)
  Pallas kernels  10.4 us (7%)
  local copies, waits for them, and re-layouts  2.93 us (2%)
    all_to_all x3, blocking collectives, trade(): return lax.all_to_all(value, axes, split_axis=0, concat_axis=0, tiled=True)  54.6 us
    all_to_all x3, waiting for transfers between devices, trade(): return lax.all_to_all(value, axes, split_axis=0, concat_axis=0, tiled=True)  35.7 us
    ppermute x3, starting transfers between devices, other_head(): return lax.ppermute(weight, ('zh', 'core', 'zl'), swaps)  16.6 us
    all_to_all x3, starting transfers between devices, trade(): return lax.all_to_all(value, axes, split_axis=0, concat_axis=0, tiled=True)  13.8 us
    pallas_call x7, Pallas kernels, call(): pl.pallas_call(kernel, out_shape=out, in_specs=specs, out_specs=outs, scr...  10.3 us
    all_gather x1, blocking collectives, body(): lax.all_gather(kv, 'zl')  4.5 us
    unnamed x18, local copies, waits for them, and re-layouts  2.9 us
  transfers between devices with their start and end apart: 6, of which 4 were waited for; matrix products, arithmetic and copies ran while one was open for 0% of the time, Pallas kernels for 3%

profile of v3, /device:TPU:1, one launch (start us, length us, event | category | flops | bytes accessed | tf_op | source)
XLA Modules:
  0.0 141.9 jit_solution(6430453524298429269)
XLA Ops:
  0.6 0.0 copy-start.2
  0.6 11.6 %collective-permute-start = (bf16[3,2048,128]{2,1,0:T(8,128)(2,1)}, bf16[3,2048,128]{2,1,0:T(8,128)(2,1)S(1)}, u32[]{:S(2)}, u32[]{:S(2)}) collective-permute-start(bf16[3,2048,128]{2,1,0:T(8,128)(2,1)} %bitcast.21), channel_id=1, source_target_pairs={{0,1},{16,401},{1,0},{17,144},{128,129},{144,17},{129,128},{145,27... | collective-permute-start | bytes 4718600 | tf_op jit(solution)/shard_map/ppermute | solution.py:237
  12.3 0.0 copy-start.3
  12.3 0.8 copy-done.3
  13.1 0.0 copy-start.5
  13.1 0.8 copy-done.5
  13.9 0.0 copy-start.7
  13.9 0.7 copy-done.7
  14.5 1.6 %shard_map.86 = bf16[8,16,2176]{2,1,0:T(8,128)(2,1)} custom-call(s32[1,32]{1,0:T(1,128)S(1)} %bitcast.32, bf16[4,4,1000]{2,1,0:T(4,128)(2,1)S(1)} %bitcast.31, bf16[1,16,2048]{2,1,0:T(8,128)(2,1)S(1)} %copy-done.3), custom_call_target="tpu_custom_call" | custom-call | bytes 97664 | tf_op jit(solution)/shard_map/pallas_call | solution.py:32
  16.2 6.8 %all-to-all-start = ((bf16[8,16,2176]{2,1,0:T(8,128)(2,1)}), bf16[8,16,2176]{2,1,0:T(8,128)(2,1)S(1)}, u32[]{:S(2)}, u32[]{:S(2)}) async-start(bf16[8,16,2176]{2,1,0:T(8,128)(2,1)} %shard_map.86), calls=%async_computation | async-start | bytes 1114112 | tf_op jit(solution)/shard_map/all_to_all | solution.py:222
  23.0 0.0 copy-done.2
  23.0 1.9 %collective-permute-start.1 = (bf16[1,128,2048]{2,1,0:T(8,128)(2,1)S(1)}, bf16[1,128,2048]{2,1,0:T(8,128)(2,1)S(1)}, u32[]{:S(2)}, u32[]{:S(2)}) collective-permute-start(bf16[1,128,2048]{2,1,0:T(8,128)(2,1)S(1)} %copy-done.2), channel_id=1, source_target_pairs={{0,1},{16,401},{1,0},{17,144},{128,129},{144,17},{129,128},{145,27... | collective-permute-start | bytes 1572872 | tf_op jit(solution)/shard_map/ppermute | solution.py:237
  24.9 11.6 %all-to-all-done.gathered_ref = bf16[8,16,2176]{2,1,0:T(8,128)(2,1)S(1)} async-done(((bf16[8,16,2176]{2,1,0:T(8,128)(2,1)}), bf16[8,16,2176]{2,1,0:T(8,128)(2,1)S(1)}, u32[]{:S(2)}, u32[]{:S(2)}) %all-to-all-start) | async-done | bytes 557088 | tf_op jit(solution)/shard_map/all_to_all | solution.py:222
  36.5 0.0 copy-start
  36.5 0.1 shard_map.87
  36.6 20.4 %all_to_all.46 = bf16[64,1,128]{2,1,0:T(2,128)(2,1)S(1)} all-to-all(bf16[64,1,128]{2,1,0:T(2,128)(2,1)S(1)} %copy.15), channel_id=1, replica_groups=mesh['zh'=4,'x'=4,'core'=2,'y'=8,'zl'=2] {'zl','zh','x','core'}, dimensions={0} | all-to-all | bytes 32768 | tf_op jit(solution)/shard_map/all_to_all | solution.py:222
  57.0 0.0 collective-permute-done.weight_ref.other_any
  57.0 0.1 shard_map.88.other_ref
  57.1 0.0 copy-done
  57.1 0.0 copy-start.6
  57.1 1.8 %shard_map.89 = (bf16[2,128,128]{2,1,0:T(8,128)(2,1)S(1)}, bf16[2,128,256]{2,1,0:T(8,128)(2,1)S(1)}, f32[8,2048]{1,0:T(8,128)S(1)}) custom-call(bf16[8,16,2176]{2,1,0:T(8,128)(2,1)S(1)} %all-to-all-done.gathered_ref, bf16[64,128]{1,0:T(8,128)(2,1)S(1)} %bitcast.29, bf16[3,2048,128]{2,1,0:T(8,128)(2,1)S(1)} %bitcast.22, ...), custom_call_target="tpu_custom_call" | custom-call | flops 402653184 | bytes 4767744 | tf_op jit(solution)/shard_map/pallas_call | solution.py:32
  59.0 4.5 %all-gather = bf16[4,128,256]{2,1,0:T(8,128)(2,1)S(1)} all-gather(bf16[2,128,256]{2,1,0:T(8,128)(2,1)S(1)} %get-tuple-element.13), channel_id=2, replica_groups=mesh['zh'=4,'x'=4,'core'=2,'y'=8,'zl'=2] {'zl'}, dimensions={0}, use_global_device_ids=true | all-gather | bytes 393216 | tf_op jit(solution)/shard_map/all_gather | solution.py:267
  63.5 0.0 copy-start.1
  63.5 0.0 copy-start.4
  63.5 0.0 collective-permute-done.1.other_ref
  63.5 0.0 copy-done.6
  63.5 2.4 %shard_map.90 = bf16[8,16,2048]{2,1,0:T(8,128)(2,1)} custom-call(f32[2,16]{1,0:T(2,128)S(1)} %copy-done.6, bf16[2,128,128]{2,1,0:T(8,128)(2,1)S(1)} %get-tuple-element.12.q_ref, bf16[2,2,128,256]{3,2,1,0:T(8,128)(2,1)S(1)} %bitcast.25, bf16[1,128,2048]{2,1,0:T(8,128)(2,1)S(1)} %copy-done.2, bf16[1,128,2048]{2,1,0:T(8,128)(2,1)S(1)} %collective-permute-done.1.other_ref), custom_call_target="tpu_custom_call" | custom-call | flops 134217728 | bytes 1376384 | tf_op jit(solution)/shard_map/pallas_call | solution.py:32
  65.9 3.5 %all-to-all-start.2 = ((bf16[8,16,2048]{2,1,0:T(8,128)(2,1)}), bf16[8,16,2048]{2,1,0:T(8,128)(2,1)S(1)}, u32[]{:S(2)}, u32[]{:S(2)}) async-start(bf16[8,16,2048]{2,1,0:T(8,128)(2,1)} %shard_map.90), calls=%async_computation.2 | async-start | bytes 1048576 | tf_op jit(solution)/shard_map/all_to_all | solution.py:222
  69.4 0.0 copy-done.1
  69.4 3.0 %collective-permute-start.2 = (bf16[3,2048,128]{2,1,0:T(8,128)(2,1)S(1)}, bf16[3,2048,128]{2,1,0:T(8,128)(2,1)}, u32[]{:S(2)}, u32[]{:S(2)}) collective-permute-start(bf16[3,2048,128]{2,1,0:T(8,128)(2,1)S(1)} %bitcast.23), channel_id=1, source_target_pairs={{0,1},{16,401},{1,0},{17,144},{128,129},{144,17},{129,128},{145,27... | collective-permute-start | bytes 4718600 | tf_op jit(solution)/shard_map/ppermute | solution.py:237
  72.4 12.4 %all-to-all-done.2.terms_ref = bf16[8,16,2048]{2,1,0:T(8,128)(2,1)S(1)} async-done(((bf16[8,16,2048]{2,1,0:T(8,128)(2,1)}), bf16[8,16,2048]{2,1,0:T(8,128)(2,1)S(1)}, u32[]{:S(2)}, u32[]{:S(2)}) %all-to-all-start.2) | async-done | bytes 524320 | tf_op jit(solution)/shard_map/all_to_all | solution.py:222
  84.8 0.0 copy-done.4
  84.8 0.9 shard_map.91
  85.8 3.5 %all-to-all-start.3 = ((bf16[8,16,2048]{2,1,0:T(8,128)(2,1)}), bf16[8,16,2048]{2,1,0:T(8,128)(2,1)S(1)}, u32[]{:S(2)}, u32[]{:S(2)}) async-start(bf16[8,16,2048]{2,1,0:T(8,128)(2,1)} %get-tuple-element.17), calls=%async_computation.3 | async-start | bytes 1048576 | tf_op jit(solution)/shard_map/all_to_all | solution.py:222
  89.3 2.6 %collective-permute-done.2.other_ref = bf16[3,2048,128]{2,1,0:T(8,128)(2,1)} collective-permute-done((bf16[3,2048,128]{2,1,0:T(8,128)(2,1)S(1)}, bf16[3,2048,128]{2,1,0:T(8,128)(2,1)}, u32[]{:S(2)}, u32[]{:S(2)}) %collective-permute-start.2) | collective-permute-done | bytes 1572896 | tf_op jit(solution)/shard_map/ppermute | solution.py:237
  91.9 11.8 %all-to-all-done.3.gathered_ref = bf16[8,16,2048]{2,1,0:T(8,128)(2,1)S(1)} async-done(((bf16[8,16,2048]{2,1,0:T(8,128)(2,1)}), bf16[8,16,2048]{2,1,0:T(8,128)(2,1)S(1)}, u32[]{:S(2)}, u32[]{:S(2)}) %all-to-all-start.3) | async-done | bytes 524320 | tf_op jit(solution)/shard_map/all_to_all | solution.py:222
  103.6 2.4 %shard_map.92 = bf16[256,384]{1,0:T(8,128)(2,1)S(1)} custom-call(bf16[8,16,2048]{2,1,0:T(8,128)(2,1)S(1)} %all-to-all-done.3.gathered_ref, f32[8,2048]{1,0:T(8,128)S(1)} %get-tuple-element.18.mod_ref, bf16[3,2048,128]{2,1,0:T(8,128)(2,1)S(1)} %bitcast.24, bf16[3,2048,128]{2,1,0:T(8,128)(2,1)} %collective-permute-done.2.other_ref), custom_call_target="tpu_custom_call" | custom-call | flops 402653184 | bytes 3735552 | tf_op jit(solution)/shard_map/pallas_call | solution.py:32
  106.0 20.6 %all_to_all.47 = bf16[32,8,384]{2,1,0:T(8,128)(2,1)S(1)} all-to-all(bf16[32,8,384]{2,1,0:T(8,128)(2,1)S(1)} %bitcast.27), channel_id=1, replica_groups=mesh['zh'=4,'x'=4,'core'=2,'y'=8,'zl'=2] {'zh','core','x'}, dimensions={0} | all-to-all | bytes 393216 | tf_op jit(solution)/shard_map/all_to_all | solution.py:222
  126.6 1.1 shard_map.93
  127.7 13.6 %all_to_all.48 = bf16[64,4,128]{2,1,0:T(4,128)(2,1)S(1)} all-to-all(bf16[64,4,128]{2,1,0:T(4,128)(2,1)S(1)} %bitcast.28), channel_id=1, replica_groups=mesh['zh'=4,'x'=4,'core'=2,'y'=8,'zl'=2] {'zh','core','zl','x'}, dimensions={0} | all-to-all | bytes 131072 | tf_op jit(solution)/shard_map/all_to_all | solution.py:222
  141.3 0.6 copy.21
  (2 shorter events, 0.0 us)
Async XLA Ops:
  0.6 22.4 %copy-start.2 = (bf16[1,128,2048]{2,1,0:T(8,128)(2,1)S(1)}, bf16[1,128,2048]{2,1,0:T(8,128)(2,1)}, u32[]{:S(2)}) copy-start(bf16[1,128,2048]{2,1,0:T(8,128)(2,1)} %own_ref) | copy-start | bytes 1572868
  0.6 56.4 %collective-permute-start = (bf16[3,2048,128]{2,1,0:T(8,128)(2,1)}, bf16[3,2048,128]{2,1,0:T(8,128)(2,1)S(1)}, u32[]{:S(2)}, u32[]{:S(2)}) collective-permute-start(bf16[3,2048,128]{2,1,0:T(8,128)(2,1)} %bitcast.21), channel_id=1, source_target_pairs={{0,1},{16,401},{1,0},{17,144},{128,129},{144,17},{129,128},{145,27... | collective-permute-start | bytes 4718600 | tf_op jit(solution)/shard_map/ppermute | solution.py:237
  12.3 0.8 copy-start.3
  13.1 0.8 copy-start.5
  13.9 0.7 copy-start.7
  16.2 20.3 %all-to-all-start = ((bf16[8,16,2176]{2,1,0:T(8,128)(2,1)}), bf16[8,16,2176]{2,1,0:T(8,128)(2,1)S(1)}, u32[]{:S(2)}, u32[]{:S(2)}) async-start(bf16[8,16,2176]{2,1,0:T(8,128)(2,1)} %shard_map.86), calls=%async_computation | async-start | bytes 1114112 | tf_op jit(solution)/shard_map/all_to_all | solution.py:222
  23.0 40.5 %collective-permute-start.1 = (bf16[1,128,2048]{2,1,0:T(8,128)(2,1)S(1)}, bf16[1,128,2048]{2,1,0:T(8,128)(2,1)S(1)}, u32[]{:S(2)}, u32[]{:S(2)}) collective-permute-start(bf16[1,128,2048]{2,1,0:T(8,128)(2,1)S(1)} %copy-done.2), channel_id=1, source_target_pairs={{0,1},{16,401},{1,0},{17,144},{128,129},{144,17},{129,128},{145,27... | collective-permute-start | bytes 1572872 | tf_op jit(solution)/shard_map/ppermute | solution.py:237
  36.5 20.6 %copy-start = (bf16[2048,3,1,128]{3,0,2,1:T(8,128)(2,1)S(1)}, bf16[2048,3,1,128]{3,0,2,1:T(8,128)(2,1)}, u32[]{:S(2)}) copy-start(bf16[2048,3,1,128]{3,0,2,1:T(8,128)(2,1)} %param.10) | copy-start | bytes 4718596
  57.1 6.3 %copy-start.6 = (f32[2,16]{1,0:T(2,128)S(1)}, f32[2,16]{1,0:T(2,128)}, u32[]{:S(2)}) copy-start(f32[2,16]{1,0:T(2,128)} %scale_ref.3) | copy-start | bytes 388
  63.5 5.9 %copy-start.1 = (bf16[2048,3,1,128]{3,0,2,1:T(8,128)(2,1)S(1)}, bf16[2048,3,1,128]{3,0,2,1:T(8,128)(2,1)}, u32[]{:S(2)}) copy-start(bf16[2048,3,1,128]{3,0,2,1:T(8,128)(2,1)} %param.12) | copy-start | bytes 4718596
  63.5 21.4 %copy-start.4 = (bf16[1,16,2048]{2,1,0:T(8,128)(2,1)S(1)}, bf16[1,16,2048]{2,1,0:T(8,128)(2,1)}, u32[]{:S(2)}) copy-start(bf16[1,16,2048]{2,1,0:T(8,128)(2,1)} %x_ref.3) | copy-start | bytes 196612
  65.9 18.9 %all-to-all-start.2 = ((bf16[8,16,2048]{2,1,0:T(8,128)(2,1)}), bf16[8,16,2048]{2,1,0:T(8,128)(2,1)S(1)}, u32[]{:S(2)}, u32[]{:S(2)}) async-start(bf16[8,16,2048]{2,1,0:T(8,128)(2,1)} %shard_map.90), calls=%async_computation.2 | async-start | bytes 1048576 | tf_op jit(solution)/shard_map/all_to_all | solution.py:222
  69.4 22.5 %collective-permute-start.2 = (bf16[3,2048,128]{2,1,0:T(8,128)(2,1)S(1)}, bf16[3,2048,128]{2,1,0:T(8,128)(2,1)}, u32[]{:S(2)}, u32[]{:S(2)}) collective-permute-start(bf16[3,2048,128]{2,1,0:T(8,128)(2,1)S(1)} %bitcast.23), channel_id=1, source_target_pairs={{0,1},{16,401},{1,0},{17,144},{128,129},{144,17},{129,128},{145,27... | collective-permute-start | bytes 4718600 | tf_op jit(solution)/shard_map/ppermute | solution.py:237
  85.8 17.9 %all-to-all-start.3 = ((bf16[8,16,2048]{2,1,0:T(8,128)(2,1)}), bf16[8,16,2048]{2,1,0:T(8,128)(2,1)S(1)}, u32[]{:S(2)}, u32[]{:S(2)}) async-start(bf16[8,16,2048]{2,1,0:T(8,128)(2,1)} %get-tuple-element.17), calls=%async_computation.3 | async-start | bytes 1048576 | tf_op jit(solution)/shard_map/all_to_all | solution.py:222

commit v4 on v3

--- a/solution.py
+++ b/solution.py
@@ -60,6 +60,8 @@
     low, high = (
         sum(gathered_ref[4 * half + i, :, 2048:2176].astype(F32) for i in range(4)) for half in range(2)
     )
+    plain = lax.axis_index("core") == 0
+    low, high = jnp.where(plain, low, high), jnp.where(plain, high, low)
     left = iota((16, 128), 1) < 64
     first = jnp.where(left, low, pltpu.roll(high, 64, 1))
     second = jnp.where(left, pltpu.roll(low, 64, 1), high)
@@ -177,6 +179,7 @@
         normed_ref[16 * j : 16 * j + 16, :] = normed_rows(gathered_ref[j], scale, shift)
     normed = normed_ref[...]
     even = lax.axis_index("zl") == 0
+    plain = lax.axis_index("core") == 0
     upper = iota((16, 8, 128), 1) < 4
     for i in range(3):
         both = dot(normed, jnp.concatenate([own_ref[i], other_ref[i]], axis=1))
@@ -187,8 +190,10 @@
         second = jnp.where(even, other, own).reshape(16, 8, 128)
         low = jnp.where(upper, first, pltpu.roll(second, 4, 1))
         high = jnp.where(upper, pltpu.roll(first, 4, 1), second)
-        rows = jnp.stack([low, high], axis=1).reshape(256, 128)
-        out_ref[:, 128 * i : 128 * i + 128] = rows.astype(BF16)
+        rows = jnp.stack([low, high], axis=1).reshape(256, 128).astype(BF16)
+        halves = rows[0:128], rows[128:256]
+        out_ref[0:128, 128 * i : 128 * i + 128] = jnp.where(plain, halves[0], halves[1])
+        out_ref[128:256, 128 * i : 128 * i + 128] = jnp.where(plain, halves[1], halves[0])
 
 
 def frame_of(index):
@@ -218,8 +223,15 @@
     def shape(*dims, dtype=BF16):
         return jax.ShapeDtypeStruct(dims, dtype)
 
-    def trade(value, axes):
-        return lax.all_to_all(value, axes, split_axis=0, concat_axis=0, tiled=True)
+    def trade(value, axes, groups=None):
+        return lax.all_to_all(
+            value, axes, split_axis=0, concat_axis=0, tiled=True, axis_index_groups=groups
+        )
+
+    ring = [list(range(8)), [8 + (y + 4) % 8 for y in range(8)]]
+
+    def trade_ring(value):
+        return trade(value, ("core", "y"), ring)
 
     swaps = []
     for z in range(8):
@@ -244,7 +256,7 @@
     far_plane = other_head(plane_weight)
     packed, mixing = lax.optimization_barrier((packed, mixing))
     far_mixing = other_head(mixing)
-    gathered = trade(packed, "y")
+    gathered = trade_ring(packed)
     own_rows = call(frame_rows_kernel, shape(64, 128), gathered)
     rows = trade(own_rows, ("zl",) + TM)
     queries, kv, mod = call(
@@ -272,11 +284,11 @@
     )
     clock_weight, terms = lax.optimization_barrier((clock_weight, terms))
     far_clock = other_head(clock_weight)
-    mixed, spread = call(mix_kernel, (shape(1, 16, 2048), shape(8, 16, 2048)), trade(terms, "y"), x)
+    mixed, spread = call(mix_kernel, (shape(1, 16, 2048), shape(8, 16, 2048)), trade_ring(terms), x)
     clock_rows = call(
         clock_project_kernel,
         shape(256, 384),
-        trade(spread, "y"),
+        trade_ring(spread),
         mod,
         clock_weight,
         far_clock,

time: 143 us -> 140 us (0.979)
  starting transfers between devices: 30.4 us -> 42.7 us
  waiting for transfers between devices: 38.3 us -> 29.8 us
  blocking collectives: 59.1 us -> 52.8 us
    all_to_all x3, starting transfers between devices: 13.8 us -> 26.2 us  [trade(): lax.all_to_all(value, axes, split_axis=0, concat_axis=0, tiled=True, axis...]
    all_to_all x3, blocking collectives: 54.6 us -> 48.3 us  [trade(): lax.all_to_all(value, axes, split_axis=0, concat_axis=0, tiled=True, axis...]
    all_to_all x3, waiting for transfers between devices: 35.7 us -> 29.6 us  [trade(): lax.all_to_all(value, axes, split_axis=0, concat_axis=0, tiled=True, axis...]
    ppermute x3, waiting for transfers between devices: 2.63 us -> 0.12 us  [other_head(): return lax.ppermute(weight, ('zh', 'core', 'zl'), swaps)]
where the time goes in v4:
time: 140 us; the launch traced here: 139 us
  blocking collectives  52.8 us (38%)
  starting transfers between devices  42.7 us (30%)
  waiting for transfers between devices  29.8 us (21%)
  Pallas kernels  10.4 us (7%)
  local copies, waits for them, and re-layouts  2.93 us (2%)
    all_to_all x3, blocking collectives, trade(): lax.all_to_all(value, axes, split_axis=0, concat_axis=0, tiled=True, axis...  48.3 us
    all_to_all x3, waiting for transfers between devices, trade(): lax.all_to_all(value, axes, split_axis=0, concat_axis=0, tiled=True, axis...  29.6 us
    all_to_all x3, starting transfers between devices, trade(): lax.all_to_all(value, axes, split_axis=0, concat_axis=0, tiled=True, axis...  26.2 us
    ppermute x3, starting transfers between devices, other_head(): return lax.ppermute(weight, ('zh', 'core', 'zl'), swaps)  16.5 us
    pallas_call x7, Pallas kernels, call(): pl.pallas_call(kernel, out_shape=out, in_specs=specs, out_specs=outs, scr...  10.3 us
    all_gather x1, blocking collectives, body(): lax.all_gather(kv, 'zl')  4.5 us
    unnamed x18, local copies, waits for them, and re-layouts  2.9 us
  transfers between devices with their start and end apart: 6, of which 4 were waited for; matrix products, arithmetic and copies ran while one was open for 0% of the time, Pallas kernels for 3%

profile of v4, /device:TPU:1, one launch (start us, length us, event | category | flops | bytes accessed | tf_op | source)
XLA Modules:
  0.0 139.3 jit_solution(17774355572783147851)
XLA Ops:
  0.6 0.0 copy-start.2
  0.6 11.6 %collective-permute-start = (bf16[3,2048,128]{2,1,0:T(8,128)(2,1)}, bf16[3,2048,128]{2,1,0:T(8,128)(2,1)S(1)}, u32[]{:S(2)}, u32[]{:S(2)}) collective-permute-start(bf16[3,2048,128]{2,1,0:T(8,128)(2,1)} %bitcast.21), channel_id=1, source_target_pairs={{0,1},{16,401},{1,0},{17,144},{128,129},{144,17},{129,128},{145,27... | collective-permute-start | bytes 4718600 | tf_op jit(solution)/shard_map/ppermute | solution.py:249
  12.3 0.0 copy-start.3
  12.3 0.8 copy-done.3
  13.1 0.0 copy-start.5
  13.1 0.8 copy-done.5
  13.9 0.0 copy-start.7
  13.9 0.7 copy-done.7
  14.5 1.6 %shard_map.86 = bf16[8,16,2176]{2,1,0:T(8,128)(2,1)} custom-call(s32[1,32]{1,0:T(1,128)S(1)} %bitcast.32, bf16[4,4,1000]{2,1,0:T(4,128)(2,1)S(1)} %bitcast.31, bf16[1,16,2048]{2,1,0:T(8,128)(2,1)S(1)} %copy-done.3), custom_call_target="tpu_custom_call" | custom-call | bytes 97664 | tf_op jit(solution)/shard_map/pallas_call | solution.py:32
  16.2 9.0 %all-to-all-start = ((bf16[8,16,2176]{2,1,0:T(8,128)(2,1)}), bf16[8,16,2176]{2,1,0:T(8,128)(2,1)S(1)}, u32[]{:S(2)}, u32[]{:S(2)}) async-start(bf16[8,16,2176]{2,1,0:T(8,128)(2,1)} %shard_map.86), calls=%async_computation | async-start | bytes 1114112 | tf_op jit(solution)/shard_map/all_to_all | solution.py:227
  25.2 0.0 copy-done.2
  25.2 1.9 %collective-permute-start.1 = (bf16[1,128,2048]{2,1,0:T(8,128)(2,1)S(1)}, bf16[1,128,2048]{2,1,0:T(8,128)(2,1)S(1)}, u32[]{:S(2)}, u32[]{:S(2)}) collective-permute-start(bf16[1,128,2048]{2,1,0:T(8,128)(2,1)S(1)} %copy-done.2), channel_id=1, source_target_pairs={{0,1},{16,401},{1,0},{17,144},{128,129},{144,17},{129,128},{145,27... | collective-permute-start | bytes 1572872 | tf_op jit(solution)/shard_map/ppermute | solution.py:249
  27.1 9.4 %all-to-all-done.gathered_ref = bf16[8,16,2176]{2,1,0:T(8,128)(2,1)S(1)} async-done(((bf16[8,16,2176]{2,1,0:T(8,128)(2,1)}), bf16[8,16,2176]{2,1,0:T(8,128)(2,1)S(1)}, u32[]{:S(2)}, u32[]{:S(2)}) %all-to-all-start) | async-done | bytes 557088 | tf_op jit(solution)/shard_map/all_to_all | solution.py:227
  36.5 0.0 copy-start
  36.5 0.1 shard_map.87
  36.6 17.5 %all_to_all.46 = bf16[64,1,128]{2,1,0:T(2,128)(2,1)S(1)} all-to-all(bf16[64,1,128]{2,1,0:T(2,128)(2,1)S(1)} %copy.15), channel_id=1, replica_groups=mesh['zh'=4,'x'=4,'core'=2,'y'=8,'zl'=2] {'zl','zh','x','core'}, dimensions={0} | all-to-all | bytes 32768 | tf_op jit(solution)/shard_map/all_to_all | solution.py:227
  54.1 0.0 collective-permute-done.weight_ref.other_any
  54.1 0.1 shard_map.88.other_ref
  54.2 0.0 copy-done
  54.2 0.0 copy-start.6
  54.2 1.8 %shard_map.89 = (bf16[2,128,128]{2,1,0:T(8,128)(2,1)S(1)}, bf16[2,128,256]{2,1,0:T(8,128)(2,1)S(1)}, f32[8,2048]{1,0:T(8,128)S(1)}) custom-call(bf16[8,16,2176]{2,1,0:T(8,128)(2,1)S(1)} %all-to-all-done.gathered_ref, bf16[64,128]{1,0:T(8,128)(2,1)S(1)} %bitcast.29, bf16[3,2048,128]{2,1,0:T(8,128)(2,1)S(1)} %bitcast.22, ...), custom_call_target="tpu_custom_call" | custom-call | flops 402653184 | bytes 4767744 | tf_op jit(solution)/shard_map/pallas_call | solution.py:32
  56.0 4.5 %all-gather = bf16[4,128,256]{2,1,0:T(8,128)(2,1)S(1)} all-gather(bf16[2,128,256]{2,1,0:T(8,128)(2,1)S(1)} %get-tuple-element.13), channel_id=2, replica_groups=mesh['zh'=4,'x'=4,'core'=2,'y'=8,'zl'=2] {'zl'}, dimensions={0}, use_global_device_ids=true | all-gather | bytes 393216 | tf_op jit(solution)/shard_map/all_gather | solution.py:279
  60.5 0.0 copy-start.1
  60.5 0.0 copy-start.4
  60.5 0.0 collective-permute-done.1.other_ref
  60.5 0.0 copy-done.6
  60.5 2.4 %shard_map.90 = bf16[8,16,2048]{2,1,0:T(8,128)(2,1)} custom-call(f32[2,16]{1,0:T(2,128)S(1)} %copy-done.6, bf16[2,128,128]{2,1,0:T(8,128)(2,1)S(1)} %get-tuple-element.12.q_ref, bf16[2,2,128,256]{3,2,1,0:T(8,128)(2,1)S(1)} %bitcast.25, bf16[1,128,2048]{2,1,0:T(8,128)(2,1)S(1)} %copy-done.2, bf16[1,128,2048]{2,1,0:T(8,128)(2,1)S(1)} %collective-permute-done.1.other_ref), custom_call_target="tpu_custom_call" | custom-call | flops 134217728 | bytes 1376384 | tf_op jit(solution)/shard_map/pallas_call | solution.py:32
  62.9 7.6 %all-to-all-start.2 = ((bf16[8,16,2048]{2,1,0:T(8,128)(2,1)}), bf16[8,16,2048]{2,1,0:T(8,128)(2,1)S(1)}, u32[]{:S(2)}, u32[]{:S(2)}) async-start(bf16[8,16,2048]{2,1,0:T(8,128)(2,1)} %shard_map.90), calls=%async_computation.2 | async-start | bytes 1048576 | tf_op jit(solution)/shard_map/all_to_all | solution.py:227
  70.5 0.0 copy-done.1
  70.5 3.0 %collective-permute-start.2 = (bf16[3,2048,128]{2,1,0:T(8,128)(2,1)S(1)}, bf16[3,2048,128]{2,1,0:T(8,128)(2,1)}, u32[]{:S(2)}, u32[]{:S(2)}) collective-permute-start(bf16[3,2048,128]{2,1,0:T(8,128)(2,1)S(1)} %bitcast.23), channel_id=1, source_target_pairs={{0,1},{16,401},{1,0},{17,144},{128,129},{144,17},{129,128},{145,27... | collective-permute-start | bytes 4718600 | tf_op jit(solution)/shard_map/ppermute | solution.py:249
  73.5 8.8 %all-to-all-done.2.terms_ref = bf16[8,16,2048]{2,1,0:T(8,128)(2,1)S(1)} async-done(((bf16[8,16,2048]{2,1,0:T(8,128)(2,1)}), bf16[8,16,2048]{2,1,0:T(8,128)(2,1)S(1)}, u32[]{:S(2)}, u32[]{:S(2)}) %all-to-all-start.2) | async-done | bytes 524320 | tf_op jit(solution)/shard_map/all_to_all | solution.py:227
  82.4 0.0 copy-done.4
  82.4 0.9 shard_map.91
  83.3 9.6 %all-to-all-start.3 = ((bf16[8,16,2048]{2,1,0:T(8,128)(2,1)}), bf16[8,16,2048]{2,1,0:T(8,128)(2,1)S(1)}, u32[]{:S(2)}, u32[]{:S(2)}) async-start(bf16[8,16,2048]{2,1,0:T(8,128)(2,1)} %get-tuple-element.17), calls=%async_computation.3 | async-start | bytes 1048576 | tf_op jit(solution)/shard_map/all_to_all | solution.py:227
  92.9 0.1 collective-permute-done.2.other_ref
  93.0 11.4 %all-to-all-done.3.gathered_ref = bf16[8,16,2048]{2,1,0:T(8,128)(2,1)S(1)} async-done(((bf16[8,16,2048]{2,1,0:T(8,128)(2,1)}), bf16[8,16,2048]{2,1,0:T(8,128)(2,1)S(1)}, u32[]{:S(2)}, u32[]{:S(2)}) %all-to-all-start.3) | async-done | bytes 524320 | tf_op jit(solution)/shard_map/all_to_all | solution.py:227
  104.4 2.4 %shard_map.92 = bf16[256,384]{1,0:T(8,128)(2,1)S(1)} custom-call(bf16[8,16,2048]{2,1,0:T(8,128)(2,1)S(1)} %all-to-all-done.3.gathered_ref, f32[8,2048]{1,0:T(8,128)S(1)} %get-tuple-element.18.mod_ref, bf16[3,2048,128]{2,1,0:T(8,128)(2,1)S(1)} %bitcast.24, bf16[3,2048,128]{2,1,0:T(8,128)(2,1)} %collective-permute-done.2.other_ref), custom_call_target="tpu_custom_call" | custom-call | flops 402653184 | bytes 3735552 | tf_op jit(solution)/shard_map/pallas_call | solution.py:32
  106.8 17.3 %all_to_all.47 = bf16[32,8,384]{2,1,0:T(8,128)(2,1)S(1)} all-to-all(bf16[32,8,384]{2,1,0:T(8,128)(2,1)S(1)} %bitcast.27), channel_id=1, replica_groups=mesh['zh'=4,'x'=4,'core'=2,'y'=8,'zl'=2] {'zh','core','x'}, dimensions={0} | all-to-all | bytes 393216 | tf_op jit(solution)/shard_map/all_to_all | solution.py:227
  124.1 1.1 shard_map.93
  125.2 13.4 %all_to_all.48 = bf16[64,4,128]{2,1,0:T(4,128)(2,1)S(1)} all-to-all(bf16[64,4,128]{2,1,0:T(4,128)(2,1)S(1)} %bitcast.28), channel_id=1, replica_groups=mesh['zh'=4,'x'=4,'core'=2,'y'=8,'zl'=2] {'zh','core','zl','x'}, dimensions={0} | all-to-all | bytes 131072 | tf_op jit(solution)/shard_map/all_to_all | solution.py:227
  138.7 0.6 copy.21
  (2 shorter events, 0.0 us)
Async XLA Ops:
  0.6 24.6 %copy-start.2 = (bf16[1,128,2048]{2,1,0:T(8,128)(2,1)S(1)}, bf16[1,128,2048]{2,1,0:T(8,128)(2,1)}, u32[]{:S(2)}) copy-start(bf16[1,128,2048]{2,1,0:T(8,128)(2,1)} %own_ref) | copy-start | bytes 1572868
  0.6 53.5 %collective-permute-start = (bf16[3,2048,128]{2,1,0:T(8,128)(2,1)}, bf16[3,2048,128]{2,1,0:T(8,128)(2,1)S(1)}, u32[]{:S(2)}, u32[]{:S(2)}) collective-permute-start(bf16[3,2048,128]{2,1,0:T(8,128)(2,1)} %bitcast.21), channel_id=1, source_target_pairs={{0,1},{16,401},{1,0},{17,144},{128,129},{144,17},{129,128},{145,27... | collective-permute-start | bytes 4718600 | tf_op jit(solution)/shard_map/ppermute | solution.py:249
  12.3 0.8 copy-start.3
  13.1 0.8 copy-start.5
  13.9 0.7 copy-start.7
  16.2 20.3 %all-to-all-start = ((bf16[8,16,2176]{2,1,0:T(8,128)(2,1)}), bf16[8,16,2176]{2,1,0:T(8,128)(2,1)S(1)}, u32[]{:S(2)}, u32[]{:S(2)}) async-start(bf16[8,16,2176]{2,1,0:T(8,128)(2,1)} %shard_map.86), calls=%async_computation | async-start | bytes 1114112 | tf_op jit(solution)/shard_map/all_to_all | solution.py:227
  25.2 35.3 %collective-permute-start.1 = (bf16[1,128,2048]{2,1,0:T(8,128)(2,1)S(1)}, bf16[1,128,2048]{2,1,0:T(8,128)(2,1)S(1)}, u32[]{:S(2)}, u32[]{:S(2)}) collective-permute-start(bf16[1,128,2048]{2,1,0:T(8,128)(2,1)S(1)} %copy-done.2), channel_id=1, source_target_pairs={{0,1},{16,401},{1,0},{17,144},{128,129},{144,17},{129,128},{145,27... | collective-permute-start | bytes 1572872 | tf_op jit(solution)/shard_map/ppermute | solution.py:249
  36.5 17.7 %copy-start = (bf16[2048,3,1,128]{3,0,2,1:T(8,128)(2,1)S(1)}, bf16[2048,3,1,128]{3,0,2,1:T(8,128)(2,1)}, u32[]{:S(2)}) copy-start(bf16[2048,3,1,128]{3,0,2,1:T(8,128)(2,1)} %param.10) | copy-start | bytes 4718596
  54.2 6.3 %copy-start.6 = (f32[2,16]{1,0:T(2,128)S(1)}, f32[2,16]{1,0:T(2,128)}, u32[]{:S(2)}) copy-start(f32[2,16]{1,0:T(2,128)} %scale_ref.3) | copy-start | bytes 388
  60.5 10.0 %copy-start.1 = (bf16[2048,3,1,128]{3,0,2,1:T(8,128)(2,1)S(1)}, bf16[2048,3,1,128]{3,0,2,1:T(8,128)(2,1)}, u32[]{:S(2)}) copy-start(bf16[2048,3,1,128]{3,0,2,1:T(8,128)(2,1)} %param.12) | copy-start | bytes 4718596
  60.5 21.9 %copy-start.4 = (bf16[1,16,2048]{2,1,0:T(8,128)(2,1)S(1)}, bf16[1,16,2048]{2,1,0:T(8,128)(2,1)}, u32[]{:S(2)}) copy-start(bf16[1,16,2048]{2,1,0:T(8,128)(2,1)} %x_ref.3) | copy-start | bytes 196612
  62.9 19.4 %all-to-all-start.2 = ((bf16[8,16,2048]{2,1,0:T(8,128)(2,1)}), bf16[8,16,2048]{2,1,0:T(8,128)(2,1)S(1)}, u32[]{:S(2)}, u32[]{:S(2)}) async-start(bf16[8,16,2048]{2,1,0:T(8,128)(2,1)} %shard_map.90), calls=%async_computation.2 | async-start | bytes 1048576 | tf_op jit(solution)/shard_map/all_to_all | solution.py:227
  70.5 22.5 %collective-permute-start.2 = (bf16[3,2048,128]{2,1,0:T(8,128)(2,1)S(1)}, bf16[3,2048,128]{2,1,0:T(8,128)(2,1)}, u32[]{:S(2)}, u32[]{:S(2)}) collective-permute-start(bf16[3,2048,128]{2,1,0:T(8,128)(2,1)S(1)} %bitcast.23), channel_id=1, source_target_pairs={{0,1},{16,401},{1,0},{17,144},{128,129},{144,17},{129,128},{145,27... | collective-permute-start | bytes 4718600 | tf_op jit(solution)/shard_map/ppermute | solution.py:249
  83.3 21.1 %all-to-all-start.3 = ((bf16[8,16,2048]{2,1,0:T(8,128)(2,1)}), bf16[8,16,2048]{2,1,0:T(8,128)(2,1)S(1)}, u32[]{:S(2)}, u32[]{:S(2)}) async-start(bf16[8,16,2048]{2,1,0:T(8,128)(2,1)} %get-tuple-element.17), calls=%async_computation.3 | async-start | bytes 1048576 | tf_op jit(solution)/shard_map/all_to_all | solution.py:227

commit v5 on v4

--- a/solution.py
+++ b/solution.py
@@ -285,6 +285,7 @@
     clock_weight, terms = lax.optimization_barrier((clock_weight, terms))
     far_clock = other_head(clock_weight)
     mixed, spread = call(mix_kernel, (shape(1, 16, 2048), shape(8, 16, 2048)), trade_ring(terms), x)
+    spread, far_clock = lax.optimization_barrier((spread, far_clock))
     clock_rows = call(
         clock_project_kernel,
         shape(256, 384),

time: 140 us -> 139 us (level)
  blocking collectives: 52.8 us -> 90.6 us
  waiting for transfers between devices: 29.8 us -> 11 us
  starting transfers between devices: 42.7 us -> 25.6 us
  Pallas kernels: 10.4 us -> 7.97 us
    all_to_all x3 -> x5, blocking collectives: 48.3 us -> 86 us  [trade(): lax.all_to_all(value, axes, split_axis=0, concat_axis=0, tiled=True, axis...]
    all_to_all x3 -> x1, waiting for transfers between devices: 29.6 us -> 9.39 us  [trade(): lax.all_to_all(value, axes, split_axis=0, concat_axis=0, tiled=True, axis...]
    all_to_all x3 -> x1, starting transfers between devices: 26.2 us -> 9 us  [trade(): lax.all_to_all(value, axes, split_axis=0, concat_axis=0, tiled=True, axis...]
    pallas_call x7, Pallas kernels: 10.3 us -> 7.91 us  [call(): pl.pallas_call(kernel, out_shape=out, in_specs=specs, out_specs=outs, scr...]
    ppermute x3, waiting for transfers between devices: 0.12 us -> 1.58 us  [other_head(): return lax.ppermute(weight, ('zh', 'core', 'zl'), swaps)]
  transfers between devices with their start and end apart: 6 -> 4, of which waited for: 4 -> 2; matrix products, arithmetic and copies ran while one was open for 0% -> 0% of each run, Pallas kernels for 3% -> 3%
where the time goes in v5:
time: 139 us
  blocking collectives  90.6 us (65%)
  starting transfers between devices  25.6 us (18%)
  waiting for transfers between devices  11 us (8%)
  Pallas kernels  7.97 us (6%)
  local copies, waits for them, and re-layouts  2.93 us (2%)
    all_to_all x5, blocking collectives, trade(): lax.all_to_all(value, axes, split_axis=0, concat_axis=0, tiled=True, axis...  86 us
    ppermute x3, starting transfers between devices, other_head(): return lax.ppermute(weight, ('zh', 'core', 'zl'), swaps)  16.6 us
    all_to_all x1, waiting for transfers between devices, trade(): lax.all_to_all(value, axes, split_axis=0, concat_axis=0, tiled=True, axis...  9.39 us
    all_to_all x1, starting transfers between devices, trade(): lax.all_to_all(value, axes, split_axis=0, concat_axis=0, tiled=True, axis...  9 us
    pallas_call x7, Pallas kernels, call(): pl.pallas_call(kernel, out_shape=out, in_specs=specs, out_specs=outs, scr...  7.91 us
    all_gather x1, blocking collectives, body(): lax.all_gather(kv, 'zl')  4.63 us
    unnamed x18, local copies, waits for them, and re-layouts  2.91 us
  transfers between devices with their start and end apart: 4, of which 2 were waited for; matrix products, arithmetic and copies ran while one was open for 0% of the time, Pallas kernels for 3%

profile of v5, /device:TPU:1, one launch (start us, length us, event | category | flops | bytes accessed | tf_op | source)
XLA Modules:
  0.0 138.8 jit_solution(159923038486991766)
XLA Ops:
  0.6 0.0 copy-start.2
  0.6 11.6 %collective-permute-start = (bf16[3,2048,128]{2,1,0:T(8,128)(2,1)}, bf16[3,2048,128]{2,1,0:T(8,128)(2,1)S(1)}, u32[]{:S(2)}, u32[]{:S(2)}) collective-permute-start(bf16[3,2048,128]{2,1,0:T(8,128)(2,1)} %bitcast.21), channel_id=1, source_target_pairs={{0,1},{16,401},{1,0},{17,144},{128,129},{144,17},{129,128},{145,27... | collective-permute-start | bytes 4718600 | tf_op jit(solution)/shard_map/ppermute | solution.py:249
  12.3 0.0 copy-start.3
  12.3 0.8 copy-done.3
  13.1 0.0 copy-start.5
  13.1 0.8 copy-done.5
  13.9 0.0 copy-start.7
  13.9 0.7 copy-done.7
  14.5 1.6 %shard_map.86 = bf16[8,16,2176]{2,1,0:T(8,128)(2,1)} custom-call(s32[1,32]{1,0:T(1,128)S(1)} %bitcast.32, bf16[4,4,1000]{2,1,0:T(4,128)(2,1)S(1)} %bitcast.31, bf16[1,16,2048]{2,1,0:T(8,128)(2,1)S(1)} %copy-done.3), custom_call_target="tpu_custom_call" | custom-call | bytes 97664 | tf_op jit(solution)/shard_map/pallas_call | solution.py:32
  16.2 9.0 %all-to-all-start = ((bf16[8,16,2176]{2,1,0:T(8,128)(2,1)}), bf16[8,16,2176]{2,1,0:T(8,128)(2,1)S(1)}, u32[]{:S(2)}, u32[]{:S(2)}) async-start(bf16[8,16,2176]{2,1,0:T(8,128)(2,1)} %shard_map.86), calls=%async_computation | async-start | bytes 1114112 | tf_op jit(solution)/shard_map/all_to_all | solution.py:227
  25.2 0.0 copy-done.2
  25.2 1.9 %collective-permute-start.1 = (bf16[1,128,2048]{2,1,0:T(8,128)(2,1)S(1)}, bf16[1,128,2048]{2,1,0:T(8,128)(2,1)S(1)}, u32[]{:S(2)}, u32[]{:S(2)}) collective-permute-start(bf16[1,128,2048]{2,1,0:T(8,128)(2,1)S(1)} %copy-done.2), channel_id=1, source_target_pairs={{0,1},{16,401},{1,0},{17,144},{128,129},{144,17},{129,128},{145,27... | collective-permute-start | bytes 1572872 | tf_op jit(solution)/shard_map/ppermute | solution.py:249
  27.1 9.4 %all-to-all-done.gathered_ref = bf16[8,16,2176]{2,1,0:T(8,128)(2,1)S(1)} async-done(((bf16[8,16,2176]{2,1,0:T(8,128)(2,1)}), bf16[8,16,2176]{2,1,0:T(8,128)(2,1)S(1)}, u32[]{:S(2)}, u32[]{:S(2)}) %all-to-all-start) | async-done | bytes 557088 | tf_op jit(solution)/shard_map/all_to_all | solution.py:227
  36.5 0.0 copy-start
  36.5 0.1 shard_map.87
  36.6 17.5 %all_to_all.46 = bf16[64,1,128]{2,1,0:T(2,128)(2,1)S(1)} all-to-all(bf16[64,1,128]{2,1,0:T(2,128)(2,1)S(1)} %copy.15), channel_id=1, replica_groups=mesh['zh'=4,'x'=4,'core'=2,'y'=8,'zl'=2] {'zl','zh','x','core'}, dimensions={0} | all-to-all | bytes 32768 | tf_op jit(solution)/shard_map/all_to_all | solution.py:227
  54.1 0.0 collective-permute-done.weight_ref.other_any
  54.1 0.1 shard_map.88.other_ref
  54.2 0.0 copy-done
  54.2 0.0 copy-start.6
  54.2 1.8 %shard_map.89 = (bf16[2,128,128]{2,1,0:T(8,128)(2,1)S(1)}, bf16[2,128,256]{2,1,0:T(8,128)(2,1)S(1)}, f32[8,2048]{1,0:T(8,128)S(1)}) custom-call(bf16[8,16,2176]{2,1,0:T(8,128)(2,1)S(1)} %all-to-all-done.gathered_ref, bf16[64,128]{1,0:T(8,128)(2,1)S(1)} %bitcast.29, bf16[3,2048,128]{2,1,0:T(8,128)(2,1)S(1)} %bitcast.22, ...), custom_call_target="tpu_custom_call" | custom-call | flops 402653184 | bytes 4767744 | tf_op jit(solution)/shard_map/pallas_call | solution.py:32
  56.0 0.0 copy-start.1
  56.0 4.6 %all-gather = bf16[4,128,256]{2,1,0:T(8,128)(2,1)S(1)} all-gather(bf16[2,128,256]{2,1,0:T(8,128)(2,1)S(1)} %get-tuple-element.15), channel_id=2, replica_groups=mesh['zh'=4,'x'=4,'core'=2,'y'=8,'zl'=2] {'zl'}, dimensions={0}, use_global_device_ids=true | all-gather | bytes 393216 | tf_op jit(solution)/shard_map/all_gather | solution.py:279
  60.7 0.0 copy-start.4
  60.7 0.0 collective-permute-done.1.other_ref
  60.7 0.0 copy-done.6
  60.7 1.6 %shard_map.90 = bf16[8,16,2048]{2,1,0:T(8,128)(2,1)S(1)} custom-call(f32[2,16]{1,0:T(2,128)S(1)} %copy-done.6, bf16[2,128,128]{2,1,0:T(8,128)(2,1)S(1)} %get-tuple-element.14.q_ref, bf16[2,2,128,256]{3,2,1,0:T(8,128)(2,1)S(1)} %bitcast.25, bf16[1,128,2048]{2,1,0:T(8,128)(2,1)S(1)} %copy-done.2, bf16[1,128,2048]{2,1,0:T(8,128)(2,1)S(1)} %collective-permute-done.1.other_ref), custom_call_target="tpu_custom_call" | custom-call | flops 134217728 | bytes 1376384 | tf_op jit(solution)/shard_map/pallas_call | solution.py:32
  62.3 0.0 copy-done.1
  62.3 3.0 %collective-permute-start.2 = (bf16[3,2048,128]{2,1,0:T(8,128)(2,1)S(1)}, bf16[3,2048,128]{2,1,0:T(8,128)(2,1)S(1)}, u32[]{:S(2)}, u32[]{:S(2)}) collective-permute-start(bf16[3,2048,128]{2,1,0:T(8,128)(2,1)S(1)} %bitcast.23), channel_id=1, source_target_pairs={{0,1},{16,401},{1,0},{17,144},{128,129},{144,17},{129,128},{145,27... | collective-permute-start | bytes 4718600 | tf_op jit(solution)/shard_map/ppermute | solution.py:249
  65.3 17.3 %all_to_all.47.terms_ref = bf16[8,16,2048]{2,1,0:T(8,128)(2,1)S(1)} all-to-all(bf16[8,16,2048]{2,1,0:T(8,128)(2,1)S(1)} %shard_map.90), channel_id=1, replica_groups={{0,2,4,6,8,10,12,14},{24,26,28,30,16,18,20,22},{1,3,5,7,9,11,13,15},{25..., dimensions={0} | all-to-all | bytes 1048576 | tf_op jit(solution)/shard_map/all_to_all | solution.py:227
  82.6 0.0 copy-done.4
  82.6 0.7 shard_map.91
  83.4 1.6 %collective-permute-done.2.other_ref = bf16[3,2048,128]{2,1,0:T(8,128)(2,1)S(1)} collective-permute-done((bf16[3,2048,128]{2,1,0:T(8,128)(2,1)S(1)}, bf16[3,2048,128]{2,1,0:T(8,128)(2,1)S(1)}, u32[]{:S(2)}, u32[]{:S(2)}) %collective-permute-start.2) | collective-permute-done | bytes 1572896 | tf_op jit(solution)/shard_map/ppermute | solution.py:249
  84.9 19.1 %all_to_all.48.gathered_ref = bf16[8,16,2048]{2,1,0:T(8,128)(2,1)S(1)} all-to-all(bf16[8,16,2048]{2,1,0:T(8,128)(2,1)S(1)} %get-tuple-element.21), channel_id=1, replica_groups={{0,2,4,6,8,10,12,14},{24,26,28,30,16,18,20,22},{1,3,5,7,9,11,13,15},{25..., dimensions={0} | all-to-all | bytes 1048576 | tf_op jit(solution)/shard_map/all_to_all | solution.py:227
  104.1 1.0 shard_map.92
  105.1 18.1 %all_to_all.49 = bf16[32,8,384]{2,1,0:T(8,128)(2,1)S(1)} all-to-all(bf16[32,8,384]{2,1,0:T(8,128)(2,1)S(1)} %bitcast.27), channel_id=1, replica_groups=mesh['zh'=4,'x'=4,'core'=2,'y'=8,'zl'=2] {'zh','core','x'}, dimensions={0} | all-to-all | bytes 393216 | tf_op jit(solution)/shard_map/all_to_all | solution.py:227
  123.2 1.1 shard_map.93
  124.3 13.9 %all_to_all.50 = bf16[64,4,128]{2,1,0:T(4,128)(2,1)S(1)} all-to-all(bf16[64,4,128]{2,1,0:T(4,128)(2,1)S(1)} %bitcast.28), channel_id=1, replica_groups=mesh['zh'=4,'x'=4,'core'=2,'y'=8,'zl'=2] {'zh','core','zl','x'}, dimensions={0} | all-to-all | bytes 131072 | tf_op jit(solution)/shard_map/all_to_all | solution.py:227
  138.2 0.6 copy.21
  (2 shorter events, 0.0 us)
Async XLA Ops:
  0.6 24.6 %copy-start.2 = (bf16[1,128,2048]{2,1,0:T(8,128)(2,1)S(1)}, bf16[1,128,2048]{2,1,0:T(8,128)(2,1)}, u32[]{:S(2)}) copy-start(bf16[1,128,2048]{2,1,0:T(8,128)(2,1)} %own_ref) | copy-start | bytes 1572868
  0.6 53.4 %collective-permute-start = (bf16[3,2048,128]{2,1,0:T(8,128)(2,1)}, bf16[3,2048,128]{2,1,0:T(8,128)(2,1)S(1)}, u32[]{:S(2)}, u32[]{:S(2)}) collective-permute-start(bf16[3,2048,128]{2,1,0:T(8,128)(2,1)} %bitcast.21), channel_id=1, source_target_pairs={{0,1},{16,401},{1,0},{17,144},{128,129},{144,17},{129,128},{145,27... | collective-permute-start | bytes 4718600 | tf_op jit(solution)/shard_map/ppermute | solution.py:249
  12.3 0.8 copy-start.3
  13.1 0.8 copy-start.5
  13.9 0.7 copy-start.7
  16.2 20.3 %all-to-all-start = ((bf16[8,16,2176]{2,1,0:T(8,128)(2,1)}), bf16[8,16,2176]{2,1,0:T(8,128)(2,1)S(1)}, u32[]{:S(2)}, u32[]{:S(2)}) async-start(bf16[8,16,2176]{2,1,0:T(8,128)(2,1)} %shard_map.86), calls=%async_computation | async-start | bytes 1114112 | tf_op jit(solution)/shard_map/all_to_all | solution.py:227
  25.2 35.5 %collective-permute-start.1 = (bf16[1,128,2048]{2,1,0:T(8,128)(2,1)S(1)}, bf16[1,128,2048]{2,1,0:T(8,128)(2,1)S(1)}, u32[]{:S(2)}, u32[]{:S(2)}) collective-permute-start(bf16[1,128,2048]{2,1,0:T(8,128)(2,1)S(1)} %copy-done.2), channel_id=1, source_target_pairs={{0,1},{16,401},{1,0},{17,144},{128,129},{144,17},{129,128},{145,27... | collective-permute-start | bytes 1572872 | tf_op jit(solution)/shard_map/ppermute | solution.py:249
  36.5 17.7 %copy-start = (bf16[2048,3,1,128]{3,0,2,1:T(8,128)(2,1)S(1)}, bf16[2048,3,1,128]{3,0,2,1:T(8,128)(2,1)}, u32[]{:S(2)}) copy-start(bf16[2048,3,1,128]{3,0,2,1:T(8,128)(2,1)} %param.10) | copy-start | bytes 4718596
  54.2 6.5 %copy-start.6 = (f32[2,16]{1,0:T(2,128)S(1)}, f32[2,16]{1,0:T(2,128)}, u32[]{:S(2)}) copy-start(f32[2,16]{1,0:T(2,128)} %scale_ref.3) | copy-start | bytes 388
  56.0 6.3 %copy-start.1 = (bf16[2048,3,1,128]{3,0,2,1:T(8,128)(2,1)S(1)}, bf16[2048,3,1,128]{3,0,2,1:T(8,128)(2,1)}, u32[]{:S(2)}) copy-start(bf16[2048,3,1,128]{3,0,2,1:T(8,128)(2,1)} %param.12) | copy-start | bytes 4718596
  60.7 22.0 %copy-start.4 = (bf16[1,16,2048]{2,1,0:T(8,128)(2,1)S(1)}, bf16[1,16,2048]{2,1,0:T(8,128)(2,1)}, u32[]{:S(2)}) copy-start(bf16[1,16,2048]{2,1,0:T(8,128)(2,1)} %x_ref.3) | copy-start | bytes 196612
  62.3 22.7 %collective-permute-start.2 = (bf16[3,2048,128]{2,1,0:T(8,128)(2,1)S(1)}, bf16[3,2048,128]{2,1,0:T(8,128)(2,1)S(1)}, u32[]{:S(2)}, u32[]{:S(2)}) collective-permute-start(bf16[3,2048,128]{2,1,0:T(8,128)(2,1)S(1)} %bitcast.23), channel_id=1, source_target_pairs={{0,1},{16,401},{1,0},{17,144},{128,129},{144,17},{129,128},{145,27... | collective-permute-start | bytes 4718600 | tf_op jit(solution)/shard_map/ppermute | solution.py:249

commit v6 on v5

--- a/solution.py
+++ b/solution.py
@@ -65,12 +65,11 @@
     left = iota((16, 128), 1) < 64
     first = jnp.where(left, low, pltpu.roll(high, 64, 1))
     second = jnp.where(left, pltpu.roll(low, 64, 1), high)
-    rows = jnp.concatenate([first, second, first, second], axis=0)
-    out_ref[...] = rows.astype(BF16)
+    out_ref[:, 0, :] = jnp.concatenate([first, second, first, second], axis=0)
 
 
 def modulation(rows_ref):
-    values = jnp.concatenate([rows_ref[0:32, :], rows_ref[32:64, :]], axis=1)
+    values = jnp.concatenate([rows_ref[0:32, 0, :], rows_ref[32:64, 0, :]], axis=1).astype(BF16)
     n = iota((256, 256), 1)
     source = ((n >> 2) & 1) * 128 + ((n >> 3) & 7) * 16 + (n >> 6) * 4 + (n & 3)
     permute = jnp.where(iota((256, 256), 0) == source, 1.0, 0.0).astype(BF16)
@@ -257,7 +256,7 @@
     packed, mixing = lax.optimization_barrier((packed, mixing))
     far_mixing = other_head(mixing)
     gathered = trade_ring(packed)
-    own_rows = call(frame_rows_kernel, shape(64, 128), gathered)
+    own_rows = call(frame_rows_kernel, shape(64, 1, 128, dtype=F32), gathered)
     rows = trade(own_rows, ("zl",) + TM)
     queries, kv, mod = call(
         plane_project_kernel,

time: 139 us -> 142 us (1.022)
  blocking collectives: 90.6 us -> 73.2 us
  waiting for transfers between devices: 11 us -> 19.8 us
  starting transfers between devices: 25.6 us -> 33.9 us
    all_to_all x5 -> x4, blocking collectives: 86 us -> 68.6 us  [trade(): lax.all_to_all(value, axes, split_axis=0, concat_axis=0, tiled=True, axis...]
    all_to_all x1 -> x2, waiting for transfers between devices: 9.39 us -> 18.3 us  [trade(): lax.all_to_all(value, axes, split_axis=0, concat_axis=0, tiled=True, axis...]
    all_to_all x1 -> x2, starting transfers between devices: 9 us -> 17.5 us  [trade(): lax.all_to_all(value, axes, split_axis=0, concat_axis=0, tiled=True, axis...]
    unnamed x18 -> x15, local copies, waits for them, and re-layouts: 2.91 us -> 4.3 us
  transfers between devices with their start and end apart: 4 -> 5, of which waited for: 2 -> 3; matrix products, arithmetic and copies ran while one was open for 0% -> 0% of each run, Pallas kernels for 3% -> 4%
where the time goes in v6:
time: 142 us; the launch traced here: 141 us
  blocking collectives  73.2 us (52%)
  starting transfers between devices  33.9 us (24%)
  waiting for transfers between devices  19.8 us (14%)
  Pallas kernels  9.3 us (7%)
  local copies, waits for them, and re-layouts  4.3 us (3%)
    all_to_all x4, blocking collectives, trade(): lax.all_to_all(value, axes, split_axis=0, concat_axis=0, tiled=True, axis...  68.6 us
    all_to_all x2, waiting for transfers between devices, trade(): lax.all_to_all(value, axes, split_axis=0, concat_axis=0, tiled=True, axis...  18.3 us
    all_to_all x2, starting transfers between devices, trade(): lax.all_to_all(value, axes, split_axis=0, concat_axis=0, tiled=True, axis...  17.5 us
    ppermute x3, starting transfers between devices, other_head(): return lax.ppermute(weight, ('zh', 'core', 'zl'), swaps)  16.4 us
    pallas_call x7, Pallas kernels, call(): pl.pallas_call(kernel, out_shape=out, in_specs=specs, out_specs=outs, scr...  9.24 us
    all_gather x1, blocking collectives, body(): lax.all_gather(kv, 'zl')  4.63 us
    unnamed x15, local copies, waits for them, and re-layouts  4.3 us
  transfers between devices with their start and end apart: 5, of which 3 were waited for; matrix products, arithmetic and copies ran while one was open for 0% of the time, Pallas kernels for 4%

profile of v6, /device:TPU:1, one launch (start us, length us, event | category | flops | bytes accessed | tf_op | source)
XLA Modules:
  0.0 141.3 jit_solution(10179449265939745311)
XLA Ops:
  0.6 11.5 %collective-permute-start = (bf16[3,2048,128]{2,1,0:T(8,128)(2,1)}, bf16[3,2048,128]{2,1,0:T(8,128)(2,1)S(1)}, u32[]{:S(2)}, u32[]{:S(2)}) collective-permute-start(bf16[3,2048,128]{2,1,0:T(8,128)(2,1)} %bitcast.17), channel_id=1, source_target_pairs={{0,1},{16,401},{1,0},{17,144},{128,129},{144,17},{129,128},{145,27... | collective-permute-start | bytes 4718600 | tf_op jit(solution)/shard_map/ppermute | solution.py:248
  12.1 0.0 copy-start.2
  12.1 0.8 copy-done.2
  13.0 0.0 copy-start.4
  13.0 0.8 copy-done.4
  13.7 0.0 copy-start.6
  13.7 0.7 copy-done.6
  14.4 1.6 %shard_map.86 = bf16[8,16,2176]{2,1,0:T(8,128)(2,1)} custom-call(s32[1,32]{1,0:T(1,128)S(1)} %bitcast.26, bf16[4,4,1000]{2,1,0:T(4,128)(2,1)S(1)} %bitcast.25, bf16[1,16,2048]{2,1,0:T(8,128)(2,1)S(1)} %copy-done.2), custom_call_target="tpu_custom_call" | custom-call | bytes 97664 | tf_op jit(solution)/shard_map/pallas_call | solution.py:32
  16.0 9.0 %all-to-all-start = ((bf16[8,16,2176]{2,1,0:T(8,128)(2,1)}), bf16[8,16,2176]{2,1,0:T(8,128)(2,1)S(1)}, u32[]{:S(2)}, u32[]{:S(2)}) async-start(bf16[8,16,2176]{2,1,0:T(8,128)(2,1)} %shard_map.86), calls=%async_computation | async-start | bytes 1114112 | tf_op jit(solution)/shard_map/all_to_all | solution.py:226
  25.0 1.9 %collective-permute-start.1 = (bf16[1,128,2048]{2,1,0:T(8,128)(2,1)}, bf16[1,128,2048]{2,1,0:T(8,128)(2,1)}, u32[]{:S(2)}, u32[]{:S(2)}) collective-permute-start(bf16[1,128,2048]{2,1,0:T(8,128)(2,1)} %own_ref), channel_id=1, source_target_pairs={{0,1},{16,401},{1,0},{17,144},{128,129},{144,17},{129,128},{145,27... | collective-permute-start | bytes 1572872 | tf_op jit(solution)/shard_map/ppermute | solution.py:248
  27.0 9.4 %all-to-all-done.gathered_ref = bf16[8,16,2176]{2,1,0:T(8,128)(2,1)S(1)} async-done(((bf16[8,16,2176]{2,1,0:T(8,128)(2,1)}), bf16[8,16,2176]{2,1,0:T(8,128)(2,1)S(1)}, u32[]{:S(2)}, u32[]{:S(2)}) %all-to-all-start) | async-done | bytes 557088 | tf_op jit(solution)/shard_map/all_to_all | solution.py:226
  36.3 0.7 shard_map.87
  37.1 8.5 %all-to-all-start.1 = ((f32[64,1,128]{2,1,0:T(1,128)}), f32[64,1,128]{2,1,0:T(1,128)S(1)}, u32[]{:S(2)}, u32[]{:S(2)}) async-start(f32[64,1,128]{2,1,0:T(1,128)} %shard_map.87), calls=%async_computation.1 | async-start | bytes 65536 | tf_op jit(solution)/shard_map/all_to_all | solution.py:226
  45.6 0.0 collective-permute-done.weight_ref.other_any
  45.6 0.1 shard_map.88.other_ref
  45.6 8.9 %all-to-all-done.1.rows_ref = f32[64,1,128]{2,1,0:T(1,128)S(1)} async-done(((f32[64,1,128]{2,1,0:T(1,128)}), f32[64,1,128]{2,1,0:T(1,128)S(1)}, u32[]{:S(2)}, u32[]{:S(2)}) %all-to-all-start.1) | async-done | bytes 32800 | tf_op jit(solution)/shard_map/all_to_all | solution.py:226
  54.5 0.0 copy-start
  54.5 1.4 copy-done
  55.9 0.0 copy-start.5
  55.9 1.8 %shard_map.89 = (bf16[2,128,128]{2,1,0:T(8,128)(2,1)S(1)}, bf16[2,128,256]{2,1,0:T(8,128)(2,1)S(1)}, f32[8,2048]{1,0:T(8,128)S(1)}) custom-call(bf16[8,16,2176]{2,1,0:T(8,128)(2,1)S(1)} %all-to-all-done.gathered_ref, f32[64,1,128]{2,1,0:T(1,128)S(1)} %all-to-all-done.1.rows_ref, bf16[3,2048,128]{2,1,0:T(8,128)(2,1)S(1)} %bitcast.18, ...), custom_call_target="tpu_custom_call" | custom-call | flops 402653184 | bytes 4784128 | tf_op jit(solution)/shard_map/pallas_call | solution.py:32
  57.8 0.0 copy-start.1
  57.8 4.6 %all-gather = bf16[4,128,256]{2,1,0:T(8,128)(2,1)S(1)} all-gather(bf16[2,128,256]{2,1,0:T(8,128)(2,1)S(1)} %get-tuple-element.15), channel_id=2, replica_groups=mesh['zh'=4,'x'=4,'core'=2,'y'=8,'zl'=2] {'zl'}, dimensions={0}, use_global_device_ids=true | all-gather | bytes 393216 | tf_op jit(solution)/shard_map/all_gather | solution.py:278
  62.4 0.0 copy-start.3
  62.4 0.0 collective-permute-done.1.other_ref
  62.4 0.0 copy-done.5
  62.4 2.3 %shard_map.90 = bf16[8,16,2048]{2,1,0:T(8,128)(2,1)S(1)} custom-call(f32[2,16]{1,0:T(2,128)S(1)} %copy-done.5, bf16[2,128,128]{2,1,0:T(8,128)(2,1)S(1)} %get-tuple-element.14.q_ref, bf16[2,2,128,256]{3,2,1,0:T(8,128)(2,1)S(1)} %bitcast.21, bf16[1,128,2048]{2,1,0:T(8,128)(2,1)} %own_ref, bf16[1,128,2048]{2,1,0:T(8,128)(2,1)} %collective-permute-done.1.other_ref), custom_call_target="tpu_custom_call" | custom-call | flops 134217728 | bytes 1376384 | tf_op jit(solution)/shard_map/pallas_call | solution.py:32
  64.7 0.0 copy-done.1
  64.7 3.0 %collective-permute-start.2 = (bf16[3,2048,128]{2,1,0:T(8,128)(2,1)S(1)}, bf16[3,2048,128]{2,1,0:T(8,128)(2,1)S(1)}, u32[]{:S(2)}, u32[]{:S(2)}) collective-permute-start(bf16[3,2048,128]{2,1,0:T(8,128)(2,1)S(1)} %bitcast.19), channel_id=1, source_target_pairs={{0,1},{16,401},{1,0},{17,144},{128,129},{144,17},{129,128},{145,27... | collective-permute-start | bytes 4718600 | tf_op jit(solution)/shard_map/ppermute | solution.py:248
  67.7 17.4 %all_to_all.40.terms_ref = bf16[8,16,2048]{2,1,0:T(8,128)(2,1)S(1)} all-to-all(bf16[8,16,2048]{2,1,0:T(8,128)(2,1)S(1)} %shard_map.90), channel_id=1, replica_groups={{0,2,4,6,8,10,12,14},{24,26,28,30,16,18,20,22},{1,3,5,7,9,11,13,15},{25..., dimensions={0} | all-to-all | bytes 1048576 | tf_op jit(solution)/shard_map/all_to_all | solution.py:226
  85.1 0.0 copy-done.3
  85.1 0.7 shard_map.91
  85.8 1.6 %collective-permute-done.2.other_ref = bf16[3,2048,128]{2,1,0:T(8,128)(2,1)S(1)} collective-permute-done((bf16[3,2048,128]{2,1,0:T(8,128)(2,1)S(1)}, bf16[3,2048,128]{2,1,0:T(8,128)(2,1)S(1)}, u32[]{:S(2)}, u32[]{:S(2)}) %collective-permute-start.2) | collective-permute-done | bytes 1572896 | tf_op jit(solution)/shard_map/ppermute | solution.py:248
  87.4 19.2 %all_to_all.41.gathered_ref = bf16[8,16,2048]{2,1,0:T(8,128)(2,1)S(1)} all-to-all(bf16[8,16,2048]{2,1,0:T(8,128)(2,1)S(1)} %get-tuple-element.21), channel_id=1, replica_groups={{0,2,4,6,8,10,12,14},{24,26,28,30,16,18,20,22},{1,3,5,7,9,11,13,15},{25..., dimensions={0} | all-to-all | bytes 1048576 | tf_op jit(solution)/shard_map/all_to_all | solution.py:226
  106.6 1.0 shard_map.92
  107.5 18.1 %all_to_all.42 = bf16[32,8,384]{2,1,0:T(8,128)(2,1)S(1)} all-to-all(bf16[32,8,384]{2,1,0:T(8,128)(2,1)S(1)} %bitcast.23), channel_id=1, replica_groups=mesh['zh'=4,'x'=4,'core'=2,'y'=8,'zl'=2] {'zh','core','x'}, dimensions={0} | all-to-all | bytes 393216 | tf_op jit(solution)/shard_map/all_to_all | solution.py:226
  125.6 1.1 shard_map.93
  126.7 13.9 %all_to_all.43 = bf16[64,4,128]{2,1,0:T(4,128)(2,1)S(1)} all-to-all(bf16[64,4,128]{2,1,0:T(4,128)(2,1)S(1)} %bitcast.24), channel_id=1, replica_groups=mesh['zh'=4,'x'=4,'core'=2,'y'=8,'zl'=2] {'zh','core','zl','x'}, dimensions={0} | all-to-all | bytes 131072 | tf_op jit(solution)/shard_map/all_to_all | solution.py:226
  140.7 0.6 copy.14
Async XLA Ops:
  0.6 44.9 %collective-permute-start = (bf16[3,2048,128]{2,1,0:T(8,128)(2,1)}, bf16[3,2048,128]{2,1,0:T(8,128)(2,1)S(1)}, u32[]{:S(2)}, u32[]{:S(2)}) collective-permute-start(bf16[3,2048,128]{2,1,0:T(8,128)(2,1)} %bitcast.17), channel_id=1, source_target_pairs={{0,1},{16,401},{1,0},{17,144},{128,129},{144,17},{129,128},{145,27... | collective-permute-start | bytes 4718600 | tf_op jit(solution)/shard_map/ppermute | solution.py:248
  12.1 0.8 copy-start.2
  13.0 0.8 copy-start.4
  13.7 0.7 copy-start.6
  16.0 20.3 %all-to-all-start = ((bf16[8,16,2176]{2,1,0:T(8,128)(2,1)}), bf16[8,16,2176]{2,1,0:T(8,128)(2,1)S(1)}, u32[]{:S(2)}, u32[]{:S(2)}) async-start(bf16[8,16,2176]{2,1,0:T(8,128)(2,1)} %shard_map.86), calls=%async_computation | async-start | bytes 1114112 | tf_op jit(solution)/shard_map/all_to_all | solution.py:226
  25.0 37.4 %collective-permute-start.1 = (bf16[1,128,2048]{2,1,0:T(8,128)(2,1)}, bf16[1,128,2048]{2,1,0:T(8,128)(2,1)}, u32[]{:S(2)}, u32[]{:S(2)}) collective-permute-start(bf16[1,128,2048]{2,1,0:T(8,128)(2,1)} %own_ref), channel_id=1, source_target_pairs={{0,1},{16,401},{1,0},{17,144},{128,129},{144,17},{129,128},{145,27... | collective-permute-start | bytes 1572872 | tf_op jit(solution)/shard_map/ppermute | solution.py:248
  37.1 17.5 %all-to-all-start.1 = ((f32[64,1,128]{2,1,0:T(1,128)}), f32[64,1,128]{2,1,0:T(1,128)S(1)}, u32[]{:S(2)}, u32[]{:S(2)}) async-start(f32[64,1,128]{2,1,0:T(1,128)} %shard_map.87), calls=%async_computation.1 | async-start | bytes 65536 | tf_op jit(solution)/shard_map/all_to_all | solution.py:226
  54.5 1.4 copy-start
  55.9 6.5 %copy-start.5 = (f32[2,16]{1,0:T(2,128)S(1)}, f32[2,16]{1,0:T(2,128)}, u32[]{:S(2)}) copy-start(f32[2,16]{1,0:T(2,128)} %scale_ref.3) | copy-start | bytes 388
  57.8 6.9 %copy-start.1 = (bf16[2048,3,1,128]{3,0,2,1:T(8,128)(2,1)S(1)}, bf16[2048,3,1,128]{3,0,2,1:T(8,128)(2,1)}, u32[]{:S(2)}) copy-start(bf16[2048,3,1,128]{3,0,2,1:T(8,128)(2,1)} %param.12) | copy-start | bytes 4718596
  62.4 22.7 %copy-start.3 = (bf16[1,16,2048]{2,1,0:T(8,128)(2,1)S(1)}, bf16[1,16,2048]{2,1,0:T(8,128)(2,1)}, u32[]{:S(2)}) copy-start(bf16[1,16,2048]{2,1,0:T(8,128)(2,1)} %x_ref.3) | copy-start | bytes 196612
  64.7 22.7 %collective-permute-start.2 = (bf16[3,2048,128]{2,1,0:T(8,128)(2,1)S(1)}, bf16[3,2048,128]{2,1,0:T(8,128)(2,1)S(1)}, u32[]{:S(2)}, u32[]{:S(2)}) collective-permute-start(bf16[3,2048,128]{2,1,0:T(8,128)(2,1)S(1)} %bitcast.19), channel_id=1, source_target_pairs={{0,1},{16,401},{1,0},{17,144},{128,129},{144,17},{129,128},{145,27... | collective-permute-start | bytes 4718600 | tf_op jit(solution)/shard_map/ppermute | solution.py:248
